TPU v7x, 512 devices: a whole 4x4x16 slice. The times are simulated.
512 devices in a mesh: seq: 64 (over y_hi, z, core), head: 8 (over y_lo, x).
Axes of the slice: x: 4, y: 4 (y_hi: 2, y_lo: 2; y = y_hi * 2 + y_lo), z: 16, core: 2. Of those that a mesh axis runs over, the one named last changes fastest.
Arguments:
- queries: bfloat16 [8192, 8192], P('seq', 'head'), may hold values from -6 to 6
- keys: bfloat16 [8192, 1024], P('seq', 'head'), may hold values from -6 to 6
- values: bfloat16 [8192, 1024], P('seq', 'head'), may hold values from -6 to 6
- layout: int32 [64], replicated, may hold values from 0 to 63, as said below
Outputs:
- attended: bfloat16 [8192, 8192], P(('seq', 'head'))
Inputs may be any that keep to these rules, and one draw needn't show every extreme that they name: `layout`: the first 32 entries hold each block below 32 once; entry 32 + i equals 63 - entry i.
All inputs are finite; a program needn't handle non-finite values.
Results may differ from a plain program's by a relative error of at most 0.007.
Values may be sent and summed in bfloat16 or wider, within the bound.
A program may use at most 128 MiB of HBM per device.

v0:
```python
import jax
import jax.numpy as jnp
from jax import lax
from jax.sharding import PartitionSpec as P

HEAD_SIZE = 128


def for_sending(array):
    return jax.tree.map(lambda a: a.astype(jnp.bfloat16) if a.dtype == jnp.float32 else a, array)


def passed_along(block, axis, distance):
    devices = range(lax.axis_size(axis))
    route = [((i - distance) % len(devices), i) for i in devices]
    return lax.ppermute(block, axis, route)


def lookup(layout, index):
    slots = jnp.arange(layout.shape[0], dtype=jnp.int32)
    return jnp.sum(jnp.where(slots == index, layout, 0))


def block_positions(layout, index, count):
    return lookup(layout, index) * count + jnp.arange(count, dtype=jnp.int32)


def split_groups(rows, kv_local, query_group):
    return rows.reshape(rows.shape[0], kv_local, query_group, HEAD_SIZE).transpose(1, 2, 0, 3)


def fresh_state(kv_local, query_group, count):
    return (
        jnp.full((kv_local, query_group, count), -1e30, jnp.float32),
        jnp.zeros((kv_local, query_group, count), jnp.float32),
        jnp.zeros((kv_local, query_group, count, HEAD_SIZE), jnp.float32),
    )


def attend(carry, q_groups, q_pos, key_rows, value_rows, k_pos):
    top, total, accum = carry
    key_heads = key_rows.reshape(key_rows.shape[0], -1, HEAD_SIZE)
    value_heads = value_rows.reshape(value_rows.shape[0], -1, HEAD_SIZE)
    score = jnp.einsum(
        "cgqd,kcd->cgqk", q_groups, key_heads, preferred_element_type=jnp.float32
    ) * HEAD_SIZE ** (-0.5)
    allowed = k_pos[None, :] <= q_pos[:, None]
    score = jnp.where(allowed, score, jnp.float32(-1e30))
    top_next = jnp.maximum(top, jnp.max(score, axis=-1))
    weight = jnp.where(allowed, jnp.exp(score - top_next[..., None]), jnp.float32(0.0))
    factor = jnp.exp(top - top_next)
    total_next = total * factor + jnp.sum(weight, axis=-1)
    accum_next = accum * factor[..., None] + jnp.einsum(
        "cgqk,kcd->cgqd",
        weight.astype(jnp.bfloat16),
        value_heads,
        preferred_element_type=jnp.float32,
    )
    return (top_next, total_next, accum_next)


def visit_one(carry, q_groups, q_pos, key_rows, value_rows, k_pos):
    return attend(carry, q_groups, q_pos, key_rows, value_rows, k_pos)


def visit(carries, query_sets, key_rows, value_rows, k_pos):
    return tuple(
        (
            visit_one(carry, entry[0], entry[1], key_rows, value_rows, k_pos)
            for carry, entry in zip(carries, query_sets)
        )
    )


def finish(carry, width):
    top, total, accum = carry
    safe_total = jnp.where(total > 0.0, total, jnp.float32(1.0))
    mixed = accum / safe_total[..., None]
    return mixed.transpose(2, 0, 1, 3).reshape(mixed.shape[2], width).astype(jnp.bfloat16)


def per_device(queries, keys, values, layout):
    count = queries.shape[0]
    kv_local = keys.shape[1] // HEAD_SIZE
    q_local = queries.shape[1] // HEAD_SIZE
    query_group = q_local // kv_local
    width = q_local * HEAD_SIZE
    seq_index = lax.axis_index("seq")
    seq_count = lax.axis_size("seq")
    own_pos = block_positions(layout, seq_index, count)
    query_sets = ((split_groups(queries, kv_local, query_group), own_pos),)
    carries = tuple((fresh_state(kv_local, query_group, entry[1].shape[0]) for entry in query_sets))
    carries = visit(carries, query_sets, keys, values, own_pos)

    def one_step(step, state):
        inner, pair = state
        pair = jax.tree.map(
            lambda part, own: part.astype(own.dtype),
            passed_along(for_sending(pair), "seq", 1),
            pair,
        )
        inner = visit(
            inner,
            query_sets,
            pair[0],
            pair[1],
            block_positions(layout, (seq_index - step) % seq_count, count),
        )
        return (inner, pair)

    carries, pair = lax.fori_loop(1, seq_count, one_step, (carries, (keys, values)))
    mixed = finish(carries[0], width)
    return lax.all_to_all(mixed, "head", split_axis=0, concat_axis=1, tiled=True)


def solution(mesh):
    placed = (P("seq", "head"), P("seq", "head"), P("seq", "head"), P())
    return jax.shard_map(
        per_device, mesh=mesh, in_specs=placed, out_specs=P(("seq", "head"), None), check_vma=False
    )
```

profile of v0, /device:TPU:1, one launch (start us, length us, event | category | flops | bytes accessed | tf_op | source)
XLA Modules:
  0.0 725.0 jit_solution(1710478303319311158)
XLA Ops:
  4.8 708.9 %while.24 = (s32[]{:T(128)}, f32[1,8,128]{2,1,0:T(8,128)S(1)}, f32[1,8,128]{2,1,0:T(8,128)S(1)}, f32[1,8,128,128]{3,2,1,0:T(8,128)S(1)}, bf16[128,128]{1,0:T(8,1...) while((s32[]{:T(128)}, f32[1,8,128]{2,1,0:T(8,128)S(1)}, ...), condition=%wide.region_7.8_spmd.clone, body=%wide.region_3.7_spmd.clone.sunk | while | flops 68570576 | bytes 3476082 | solution.py:111
  4.8 4.9 collective-permute-start
  22.0 4.4 collective-permute-done
  34.1 3.6 collective-permute-done
  56.5 3.6 collective-permute-done
  79.0 3.6 collective-permute-done
  101.4 3.6 collective-permute-done
  123.9 3.6 collective-permute-done
  146.4 3.6 collective-permute-done
  168.8 3.6 collective-permute-done
  191.3 3.6 collective-permute-done
  213.7 3.6 collective-permute-done
  236.2 3.6 collective-permute-done
  258.7 3.6 collective-permute-done
  281.1 3.6 collective-permute-done
  303.6 3.6 collective-permute-done
  326.0 3.6 collective-permute-done
  348.5 3.6 collective-permute-done
  370.9 3.6 collective-permute-done
  393.4 3.6 collective-permute-done
  415.9 3.6 collective-permute-done
  438.3 3.6 collective-permute-done
  618.0 3.6 collective-permute-done
  714.3 10.0 %all_to_all.16 = bf16[8,16,1024]{2,1,0:T(8,128)(2,1)S(1)} all-to-all(bf16[8,16,1024]{2,1,0:T(8,128)(2,1)S(1)} %convert_element_type.28), channel_id=1, replica_groups=mesh['seq'=64,'head'=8] {'head'}, dimensions={0} | all-to-all | bytes 524288 | tf_op jit(solution)/shard_map/all_to_all | solution.py:113
  (944 shorter events, 586.1 us)
Async XLA Ops:
  4.8 9.5 %collective-permute-start = (bf16[128,128]{1,0:T(8,128)(2,1)S(1)}, bf16[128,128]{1,0:T(8,128)(2,1)S(1)}, u32[]{:S(2)}, u32[]{:S(2)}) collective-permute-start(bf16[128,128]{1,0:T(8,128)(2,1)S(1)} %get-tuple-element.417), channel_id=1, source_target_pairs={{504,0},{0,8},{8,16},{16,24},{24,32},{32,40},{40,48},{48,56},{56,6... | collective-permute-start | bytes 98312 | tf_op jit(solution)/shard_map/while/body/eval_jaxpr/ppermute | solution.py:16
  16.7 9.7 %collective-permute-start = (bf16[128,128]{1,0:T(8,128)(2,1)S(1)}, bf16[128,128]{1,0:T(8,128)(2,1)S(1)}, u32[]{:S(2)}, u32[]{:S(2)}) collective-permute-start(bf16[128,128]{1,0:T(8,128)(2,1)S(1)} %get-tuple-element.417), channel_id=1, source_target_pairs={{504,0},{0,8},{8,16},{16,24},{24,32},{32,40},{40,48},{48,56},{56,6... | collective-permute-start | bytes 98312 | tf_op jit(solution)/shard_map/while/body/eval_jaxpr/ppermute | solution.py:16
  18.6 9.7 %collective-permute-start.1 = (bf16[128,128]{1,0:T(8,128)(2,1)S(1)}, bf16[128,128]{1,0:T(8,128)(2,1)S(1)}, u32[]{:S(2)}, u32[]{:S(2)}) collective-permute-start(bf16[128,128]{1,0:T(8,128)(2,1)S(1)} %get-tuple-element.418), channel_id=1, source_target_pairs={{504,0},{0,8},{8,16},{16,24},{24,32},{32,40},{40,48},{48,56},{56,6... | collective-permute-start | bytes 98312 | tf_op jit(solution)/shard_map/while/body/eval_jaxpr/ppermute | solution.py:16
  28.8 8.8 %collective-permute-start = (bf16[128,128]{1,0:T(8,128)(2,1)S(1)}, bf16[128,128]{1,0:T(8,128)(2,1)S(1)}, u32[]{:S(2)}, u32[]{:S(2)}) collective-permute-start(bf16[128,128]{1,0:T(8,128)(2,1)S(1)} %get-tuple-element.417), channel_id=1, source_target_pairs={{504,0},{0,8},{8,16},{16,24},{24,32},{32,40},{40,48},{48,56},{56,6... | collective-permute-start | bytes 98312 | tf_op jit(solution)/shard_map/while/body/eval_jaxpr/ppermute | solution.py:16
  30.7 8.8 %collective-permute-start.1 = (bf16[128,128]{1,0:T(8,128)(2,1)S(1)}, bf16[128,128]{1,0:T(8,128)(2,1)S(1)}, u32[]{:S(2)}, u32[]{:S(2)}) collective-permute-start(bf16[128,128]{1,0:T(8,128)(2,1)S(1)} %get-tuple-element.418), channel_id=1, source_target_pairs={{504,0},{0,8},{8,16},{16,24},{24,32},{32,40},{40,48},{48,56},{56,6... | collective-permute-start | bytes 98312 | tf_op jit(solution)/shard_map/while/body/eval_jaxpr/ppermute | solution.py:16
  51.2 8.8 %collective-permute-start = (bf16[128,128]{1,0:T(8,128)(2,1)S(1)}, bf16[128,128]{1,0:T(8,128)(2,1)S(1)}, u32[]{:S(2)}, u32[]{:S(2)}) collective-permute-start(bf16[128,128]{1,0:T(8,128)(2,1)S(1)} %get-tuple-element.417), channel_id=1, source_target_pairs={{504,0},{0,8},{8,16},{16,24},{24,32},{32,40},{40,48},{48,56},{56,6... | collective-permute-start | bytes 98312 | tf_op jit(solution)/shard_map/while/body/eval_jaxpr/ppermute | solution.py:16
  53.2 8.8 %collective-permute-start.1 = (bf16[128,128]{1,0:T(8,128)(2,1)S(1)}, bf16[128,128]{1,0:T(8,128)(2,1)S(1)}, u32[]{:S(2)}, u32[]{:S(2)}) collective-permute-start(bf16[128,128]{1,0:T(8,128)(2,1)S(1)} %get-tuple-element.418), channel_id=1, source_target_pairs={{504,0},{0,8},{8,16},{16,24},{24,32},{32,40},{40,48},{48,56},{56,6... | collective-permute-start | bytes 98312 | tf_op jit(solution)/shard_map/while/body/eval_jaxpr/ppermute | solution.py:16
  73.7 8.8 %collective-permute-start = (bf16[128,128]{1,0:T(8,128)(2,1)S(1)}, bf16[128,128]{1,0:T(8,128)(2,1)S(1)}, u32[]{:S(2)}, u32[]{:S(2)}) collective-permute-start(bf16[128,128]{1,0:T(8,128)(2,1)S(1)} %get-tuple-element.417), channel_id=1, source_target_pairs={{504,0},{0,8},{8,16},{16,24},{24,32},{32,40},{40,48},{48,56},{56,6... | collective-permute-start | bytes 98312 | tf_op jit(solution)/shard_map/while/body/eval_jaxpr/ppermute | solution.py:16
  75.6 8.8 %collective-permute-start.1 = (bf16[128,128]{1,0:T(8,128)(2,1)S(1)}, bf16[128,128]{1,0:T(8,128)(2,1)S(1)}, u32[]{:S(2)}, u32[]{:S(2)}) collective-permute-start(bf16[128,128]{1,0:T(8,128)(2,1)S(1)} %get-tuple-element.418), channel_id=1, source_target_pairs={{504,0},{0,8},{8,16},{16,24},{24,32},{32,40},{40,48},{48,56},{56,6... | collective-permute-start | bytes 98312 | tf_op jit(solution)/shard_map/while/body/eval_jaxpr/ppermute | solution.py:16
  96.2 8.8 %collective-permute-start = (bf16[128,128]{1,0:T(8,128)(2,1)S(1)}, bf16[128,128]{1,0:T(8,128)(2,1)S(1)}, u32[]{:S(2)}, u32[]{:S(2)}) collective-permute-start(bf16[128,128]{1,0:T(8,128)(2,1)S(1)} %get-tuple-element.417), channel_id=1, source_target_pairs={{504,0},{0,8},{8,16},{16,24},{24,32},{32,40},{40,48},{48,56},{56,6... | collective-permute-start | bytes 98312 | tf_op jit(solution)/shard_map/while/body/eval_jaxpr/ppermute | solution.py:16
  98.1 8.8 %collective-permute-start.1 = (bf16[128,128]{1,0:T(8,128)(2,1)S(1)}, bf16[128,128]{1,0:T(8,128)(2,1)S(1)}, u32[]{:S(2)}, u32[]{:S(2)}) collective-permute-start(bf16[128,128]{1,0:T(8,128)(2,1)S(1)} %get-tuple-element.418), channel_id=1, source_target_pairs={{504,0},{0,8},{8,16},{16,24},{24,32},{32,40},{40,48},{48,56},{56,6... | collective-permute-start | bytes 98312 | tf_op jit(solution)/shard_map/while/body/eval_jaxpr/ppermute | solution.py:16
  118.6 8.8 %collective-permute-start = (bf16[128,128]{1,0:T(8,128)(2,1)S(1)}, bf16[128,128]{1,0:T(8,128)(2,1)S(1)}, u32[]{:S(2)}, u32[]{:S(2)}) collective-permute-start(bf16[128,128]{1,0:T(8,128)(2,1)S(1)} %get-tuple-element.417), channel_id=1, source_target_pairs={{504,0},{0,8},{8,16},{16,24},{24,32},{32,40},{40,48},{48,56},{56,6... | collective-permute-start | bytes 98312 | tf_op jit(solution)/shard_map/while/body/eval_jaxpr/ppermute | solution.py:16
  120.5 8.8 %collective-permute-start.1 = (bf16[128,128]{1,0:T(8,128)(2,1)S(1)}, bf16[128,128]{1,0:T(8,128)(2,1)S(1)}, u32[]{:S(2)}, u32[]{:S(2)}) collective-permute-start(bf16[128,128]{1,0:T(8,128)(2,1)S(1)} %get-tuple-element.418), channel_id=1, source_target_pairs={{504,0},{0,8},{8,16},{16,24},{24,32},{32,40},{40,48},{48,56},{56,6... | collective-permute-start | bytes 98312 | tf_op jit(solution)/shard_map/while/body/eval_jaxpr/ppermute | solution.py:16
  141.1 8.8 %collective-permute-start = (bf16[128,128]{1,0:T(8,128)(2,1)S(1)}, bf16[128,128]{1,0:T(8,128)(2,1)S(1)}, u32[]{:S(2)}, u32[]{:S(2)}) collective-permute-start(bf16[128,128]{1,0:T(8,128)(2,1)S(1)} %get-tuple-element.417), channel_id=1, source_target_pairs={{504,0},{0,8},{8,16},{16,24},{24,32},{32,40},{40,48},{48,56},{56,6... | collective-permute-start | bytes 98312 | tf_op jit(solution)/shard_map/while/body/eval_jaxpr/ppermute | solution.py:16
  143.0 8.8 %collective-permute-start.1 = (bf16[128,128]{1,0:T(8,128)(2,1)S(1)}, bf16[128,128]{1,0:T(8,128)(2,1)S(1)}, u32[]{:S(2)}, u32[]{:S(2)}) collective-permute-start(bf16[128,128]{1,0:T(8,128)(2,1)S(1)} %get-tuple-element.418), channel_id=1, source_target_pairs={{504,0},{0,8},{8,16},{16,24},{24,32},{32,40},{40,48},{48,56},{56,6... | collective-permute-start | bytes 98312 | tf_op jit(solution)/shard_map/while/body/eval_jaxpr/ppermute | solution.py:16
  163.5 8.8 %collective-permute-start = (bf16[128,128]{1,0:T(8,128)(2,1)S(1)}, bf16[128,128]{1,0:T(8,128)(2,1)S(1)}, u32[]{:S(2)}, u32[]{:S(2)}) collective-permute-start(bf16[128,128]{1,0:T(8,128)(2,1)S(1)} %get-tuple-element.417), channel_id=1, source_target_pairs={{504,0},{0,8},{8,16},{16,24},{24,32},{32,40},{40,48},{48,56},{56,6... | collective-permute-start | bytes 98312 | tf_op jit(solution)/shard_map/while/body/eval_jaxpr/ppermute | solution.py:16
  165.5 8.8 %collective-permute-start.1 = (bf16[128,128]{1,0:T(8,128)(2,1)S(1)}, bf16[128,128]{1,0:T(8,128)(2,1)S(1)}, u32[]{:S(2)}, u32[]{:S(2)}) collective-permute-start(bf16[128,128]{1,0:T(8,128)(2,1)S(1)} %get-tuple-element.418), channel_id=1, source_target_pairs={{504,0},{0,8},{8,16},{16,24},{24,32},{32,40},{40,48},{48,56},{56,6... | collective-permute-start | bytes 98312 | tf_op jit(solution)/shard_map/while/body/eval_jaxpr/ppermute | solution.py:16
  186.0 8.8 %collective-permute-start = (bf16[128,128]{1,0:T(8,128)(2,1)S(1)}, bf16[128,128]{1,0:T(8,128)(2,1)S(1)}, u32[]{:S(2)}, u32[]{:S(2)}) collective-permute-start(bf16[128,128]{1,0:T(8,128)(2,1)S(1)} %get-tuple-element.417), channel_id=1, source_target_pairs={{504,0},{0,8},{8,16},{16,24},{24,32},{32,40},{40,48},{48,56},{56,6... | collective-permute-start | bytes 98312 | tf_op jit(solution)/shard_map/while/body/eval_jaxpr/ppermute | solution.py:16
  187.9 8.8 %collective-permute-start.1 = (bf16[128,128]{1,0:T(8,128)(2,1)S(1)}, bf16[128,128]{1,0:T(8,128)(2,1)S(1)}, u32[]{:S(2)}, u32[]{:S(2)}) collective-permute-start(bf16[128,128]{1,0:T(8,128)(2,1)S(1)} %get-tuple-element.418), channel_id=1, source_target_pairs={{504,0},{0,8},{8,16},{16,24},{24,32},{32,40},{40,48},{48,56},{56,6... | collective-permute-start | bytes 98312 | tf_op jit(solution)/shard_map/while/body/eval_jaxpr/ppermute | solution.py:16
  208.5 8.8 %collective-permute-start = (bf16[128,128]{1,0:T(8,128)(2,1)S(1)}, bf16[128,128]{1,0:T(8,128)(2,1)S(1)}, u32[]{:S(2)}, u32[]{:S(2)}) collective-permute-start(bf16[128,128]{1,0:T(8,128)(2,1)S(1)} %get-tuple-element.417), channel_id=1, source_target_pairs={{504,0},{0,8},{8,16},{16,24},{24,32},{32,40},{40,48},{48,56},{56,6... | collective-permute-start | bytes 98312 | tf_op jit(solution)/shard_map/while/body/eval_jaxpr/ppermute | solution.py:16
  210.4 8.8 %collective-permute-start.1 = (bf16[128,128]{1,0:T(8,128)(2,1)S(1)}, bf16[128,128]{1,0:T(8,128)(2,1)S(1)}, u32[]{:S(2)}, u32[]{:S(2)}) collective-permute-start(bf16[128,128]{1,0:T(8,128)(2,1)S(1)} %get-tuple-element.418), channel_id=1, source_target_pairs={{504,0},{0,8},{8,16},{16,24},{24,32},{32,40},{40,48},{48,56},{56,6... | collective-permute-start | bytes 98312 | tf_op jit(solution)/shard_map/while/body/eval_jaxpr/ppermute | solution.py:16
  230.9 8.8 %collective-permute-start = (bf16[128,128]{1,0:T(8,128)(2,1)S(1)}, bf16[128,128]{1,0:T(8,128)(2,1)S(1)}, u32[]{:S(2)}, u32[]{:S(2)}) collective-permute-start(bf16[128,128]{1,0:T(8,128)(2,1)S(1)} %get-tuple-element.417), channel_id=1, source_target_pairs={{504,0},{0,8},{8,16},{16,24},{24,32},{32,40},{40,48},{48,56},{56,6... | collective-permute-start | bytes 98312 | tf_op jit(solution)/shard_map/while/body/eval_jaxpr/ppermute | solution.py:16
  367.6 8.8 %collective-permute-start.1 = (bf16[128,128]{1,0:T(8,128)(2,1)S(1)}, bf16[128,128]{1,0:T(8,128)(2,1)S(1)}, u32[]{:S(2)}, u32[]{:S(2)}) collective-permute-start(bf16[128,128]{1,0:T(8,128)(2,1)S(1)} %get-tuple-element.418), channel_id=1, source_target_pairs={{504,0},{0,8},{8,16},{16,24},{24,32},{32,40},{40,48},{48,56},{56,6... | collective-permute-start | bytes 98312 | tf_op jit(solution)/shard_map/while/body/eval_jaxpr/ppermute | solution.py:16
  612.7 8.8 %collective-permute-start = (bf16[128,128]{1,0:T(8,128)(2,1)S(1)}, bf16[128,128]{1,0:T(8,128)(2,1)S(1)}, u32[]{:S(2)}, u32[]{:S(2)}) collective-permute-start(bf16[128,128]{1,0:T(8,128)(2,1)S(1)} %get-tuple-element.417), channel_id=1, source_target_pairs={{504,0},{0,8},{8,16},{16,24},{24,32},{32,40},{40,48},{48,56},{56,6... | collective-permute-start | bytes 98312 | tf_op jit(solution)/shard_map/while/body/eval_jaxpr/ppermute | solution.py:16
  (104 other events, 901.5 us)
where the time goes:
time: 738 us; the launch traced here: 725 us
  waiting for transfers between devices  319 us (43%)
  starting transfers between devices  245 us (33%)
  other arithmetic  56 us (8%)
  loops' own time  47.5 us (6%)
  matrix products  42.6 us (6%)
  blocking collectives  9.98 us (1%)
    ppermute x126, waiting for transfers between devices, passed_along(): return lax.ppermute(block, axis, route)  319 us
    ppermute x126, starting transfers between devices, passed_along(): return lax.ppermute(block, axis, route)  245 us
    another operation x1, loops' own time, per_device(): lax.fori_loop(1, seq_count, one_step, (carries, (keys, values)))  47.5 us
    reduce_sum x64, other arithmetic, lookup(): return jnp.sum(jnp.where(slots == index, layout, 0))  42.1 us
    dot_general x64, matrix products, attend(): jnp.einsum('cgqk,kcd->cgqd', weight.astype(jnp.bfloat16), value_heads, pr...  27.5 us
    dot_general x64, matrix products, attend(): jnp.einsum('cgqd,kcd->cgqk', q_groups, key_heads, preferred_element_type=...  15.2 us
  transfers between devices with their start and end apart: 126, of which 126 were waited for; matrix products, arithmetic and copies ran while one was open for 10% of the time, Pallas kernels for 0%

commit v1 on v0

v1 whole, which is shorter than its diff:
```python
import math

import jax
import jax.numpy as jnp
from jax import lax
from jax.experimental import pallas as pl
from jax.experimental.pallas import tpu as pltpu
from jax.sharding import PartitionSpec as P


HEAD_SIZE = 128
MESH = pl.DeviceIdType.MESH
EMPTY = -1e30
SCALE = math.log2(math.e) / math.sqrt(HEAD_SIZE)
TILE = 4
CHUNKS = 2


def kernel(
    nz, heads, layout_ref, q_ref, k_ref, v_ref, out_ref,
    kv, qx, relay, qs, m_s, al_s, out_send, out_recv, stat_send, stat_recv, lse, pick, limit, place,
    ring_send, ring_recv, share_send, share_recv, cross_send, cross_recv,
    first_send, first_recv, second_send, second_recv, o_send, o_recv,
):
    tok, width = q_ref.shape
    group = width // HEAD_SIZE
    per_chunk = group // CHUNKS
    rows = per_chunk * tok
    seq, h = lax.axis_index("seq"), lax.axis_index("head")
    plane, z, core = seq // (2 * nz), (seq // 2) % nz, seq % 2
    nx = heads // 2
    y_lo, x = h // nx, h % nx

    def at(p, zz, cc):
        return (p * nz + zz) * 2 + cc

    right, left = (at(plane, (z + 1) % nz, core), h), (at(plane, (z + nz - 1) % nz, core), h)
    sibling, cross = (at(plane, z, 1 - core), h), (at(1 - plane, z, 1 - core), h)
    above = (at((plane + y_lo) % 2, z, core), (1 - y_lo) * nx + x)
    below = (at((plane + 1 - y_lo) % 2, z, core), (1 - y_lo) * nx + x)

    def outward(e):
        return (plane + e // heads) % 2, (h + e % heads) % heads

    def send(src, dst, send_sem, recv_sem, device):
        return pltpu.make_async_remote_copy(
            src_ref=src, dst_ref=dst, send_sem=send_sem, recv_sem=recv_sem, device_id=device, device_id_type=MESH
        )

    barrier = pltpu.get_barrier_semaphore()
    for device in (right, left, sibling, cross):
        pl.semaphore_signal(barrier, inc=1, device_id=device, device_id_type=MESH)
    for e in range(1, 2 * heads):
        p, j = outward(e)
        pl.semaphore_signal(barrier, inc=1, device_id=(at(p, z, core), j), device_id_type=MESH)
    pl.semaphore_wait(barrier, 4 + 2 * heads - 1)

    def ring(way, d, g):
        src, dst, device = (d - 1, d, right) if way == 0 else ((nz - d + 1) % nz, nz - d, left)
        return send(kv.at[src, core, g], kv.at[dst, core, g], ring_send.at[dst, g], ring_recv.at[dst, g], device)

    def share(slot, g):
        return send(kv.at[slot, core, g], kv.at[slot, core, g], share_send.at[slot, g], share_recv.at[slot, g], sibling)

    def shared(slot, g):
        ref = kv.at[slot, 1 - core, g]
        return send(ref, ref, share_send.at[slot, g], share_recv.at[slot, g], sibling)

    def exchange(g):
        return send((k_ref, v_ref)[g], kv.at[0, 1 - core, g], cross_send.at[g], cross_recv.at[g], cross)

    def exchanged(g):
        return send((k_ref, v_ref)[g], kv.at[0, core, g], cross_send.at[g], cross_recv.at[g], cross)

    half, strip = width // 2, tok // 2

    def first(way, r):
        src = q_ref.at[pl.ds(r * strip, strip), pl.ds(way * half, half)]
        return send(src, relay.at[way, r], first_send.at[way, r], first_recv.at[way, r], (above, below)[way])

    def second(way, r):
        dst = qx.at[pl.ds(r * strip, strip), pl.ds(way * half, half)]
        return send(relay.at[way, r], dst, second_send.at[way, r], second_recv.at[way, r], (above, below)[way])

    @pl.when(core != plane)
    def _():
        for g in range(2):
            exchange(g).start()

    @pl.when(core == plane)
    def _():
        kv[0, core, 0] = k_ref[...]
        kv[0, core, 1] = v_ref[...]

    for r in range(2):
        for way in range(2):
            first(way, r).start()

    for g in range(2):

        @pl.when(core != plane)
        def _():
            exchanged(g).wait_recv()

        for way in range(2):
            ring(way, 1, g).start()
        share(0, g).start()

    tiles = nz // TILE + 1
    own = layout_ref[2 * z + core]
    below_count = jnp.int32(0)
    for i in range(nz):
        below_count += (layout_ref[2 * ((z + nz - i) % nz) + plane] <= own).astype(jnp.int32)
    low_tiles = (below_count + TILE - 1) // TILE
    low_next, high_next = jnp.int32(0), low_tiles * TILE
    for i in range(nz):
        position = layout_ref[2 * ((z + nz - i) % nz) + plane]
        is_low, is_high = position <= own, position >= own
        place[0, i] = jnp.where(is_low, low_next, -1)
        place[1, i] = jnp.where(is_high, high_next, -1)
        place[2, i] = jnp.where(position == own, 0, tok)
        low_next += is_low.astype(jnp.int32)
        high_next += is_high.astype(jnp.int32)

    def order(t, _):
        slot, bound = jnp.int32(0), jnp.int32(-tok)
        for i in range(nz):
            here = (place[0, i] == t) | (place[1, i] == t)
            slot = jnp.where(here, i, slot)
            bound = jnp.where(here, place[2, i], bound)
        pick[t] = slot
        limit[t] = bound
        return 0

    lax.fori_loop(0, tiles * TILE, order, 0)

    def scaled(target, ref):
        for head in range(group):
            block = ref[:, head * HEAD_SIZE:(head + 1) * HEAD_SIZE].astype(jnp.float32) * SCALE
            chunk, start = head // per_chunk, (head % per_chunk) * tok
            qs[target, chunk, start:start + tok, :] = block.astype(jnp.bfloat16)

    scaled(plane, q_ref)

    ones = jnp.ones((TILE * tok, HEAD_SIZE), jnp.bfloat16)

    def update(q, keys, values, m, al, bounds):
        score = lax.dot_general(q, keys, (((1,), (1,)), ((), ())), preferred_element_type=jnp.float32)
        if bounds is not None:
            ahead = lax.broadcasted_iota(jnp.int32, (rows, tok), 1) - lax.rem(
                lax.broadcasted_iota(jnp.int32, (rows, tok), 0), tok
            )
            score = jnp.concatenate(
                [
                    jnp.where(ahead <= bounds[j], score[:, j * tok:(j + 1) * tok], EMPTY)
                    for j in range(TILE)
                ],
                axis=1,
            )
        m_next = jnp.maximum(m, jnp.max(score, axis=1, keepdims=True))
        weight = jnp.exp2(score - jnp.concatenate([m_next] * TILE, axis=1)).astype(jnp.bfloat16)
        mixed = jnp.dot(weight, jnp.concatenate([values, ones], axis=1), preferred_element_type=jnp.float32)
        factor = jnp.exp2(m - m_next)
        return m_next, al * jnp.concatenate([factor, factor], axis=1) + mixed

    def first_part(slots, fresh):
        keys = jnp.concatenate([kv[i, 0, 0] for i in slots], axis=0)
        values = jnp.concatenate([kv[i, 0, 1] for i in slots], axis=0)

        def chunk_step(chunk, _):
            if fresh:
                m = jnp.full((rows, HEAD_SIZE), EMPTY, jnp.float32)
                al = jnp.zeros((rows, 2 * HEAD_SIZE), jnp.float32)
                m_s[0, chunk] = m
                al_s[0, chunk] = al
            else:
                m, al = m_s[1, chunk], al_s[1, chunk]
            m, al = update(qs[1, chunk], keys, values, m, al, None)
            m_s[1, chunk] = m
            al_s[1, chunk] = al
            return 0

        lax.fori_loop(0, CHUNKS, chunk_step, 0)

    arrival = [0] + [i for d in range(1, nz // 2) for i in (d, nz - d)] + [nz // 2]
    parts = [arrival[i:i + TILE] for i in range(0, nz, TILE)]
    last = nz // 2

    def run_part(index):
        for slot in parts[index]:
            for g in range(2):
                shared(slot, g).wait_recv()
        first_part(parts[index], index == 0)

    start_at = last - len(parts) + 1
    for d in range(1, last + 1):
        for g in range(2):
            if d < last:
                for way in range(2):
                    ring(way, d, g).wait_recv()
                    if d + 1 < last:
                        ring(way, d + 1, g).start()
                    else:

                        @pl.when(core == way)
                        def _():
                            ring(way, d + 1, g).start()

                    share(d if way == 0 else nz - d, g).start()
            else:
                ring(0, d, g).wait_recv()
                share(d, g).start()
        if d <= 2:
            for way in range(2):
                first(way, d - 1).wait_recv()
                second(way, d - 1).start()
        if d == start_at - 1:
            for r in range(2):
                for way in range(2):
                    second(way, r).wait_recv()
            scaled(1 - plane, qx)
        if d >= start_at:
            run_part(d - start_at)

    lane = lax.broadcasted_iota(jnp.int32, (tok, HEAD_SIZE), 1)
    piece = tok // heads

    def spread(buffer, landing, index):
        for e in range(1, 2 * heads):
            p, j = outward(e)
            send(
                buffer.at[p * heads + j], landing.at[plane * heads + h], o_send.at[index], o_recv.at[index],
                (at(p, z, core), j),
            ).start()
        mine = plane * heads + h
        pltpu.make_async_copy(buffer.at[mine], landing.at[mine], o_recv.at[index]).start()

    def chunk_step(chunk, _):
        for t in range(tiles):
            is_low = t < low_tiles
            side = jnp.where(is_low, 0, 1)
            before = jnp.where(t == low_tiles, 1, 0 if t == 0 else t + 1)
            slots = [pick[t * TILE + j] for j in range(TILE)]
            bounds = [limit[t * TILE + j] for j in range(TILE)]
            keys = jnp.concatenate([kv[i, side, 0] for i in slots], axis=0)
            values = jnp.concatenate([kv[i, side, 1] for i in slots], axis=0)
            m, al = update(qs[side, chunk], keys, values, m_s[before, chunk], al_s[before, chunk], bounds)
            m_s[2 + t, chunk] = m
            al_s[2 + t, chunk] = al
        for side in range(2):
            end = jnp.where(low_tiles == 0, 0, low_tiles + 1) if side == 0 else tiles + 1
            m, al = m_s[end, chunk], al_s[end, chunk]
            total = al[:, HEAD_SIZE:]
            some = total > 0.0
            safe = jnp.where(some, total, 1.0)
            mixed = (al[:, :HEAD_SIZE] / safe).astype(jnp.bfloat16)
            level = jnp.where(some, m + jnp.log2(safe), EMPTY)
            for k in range(per_chunk):
                block = mixed[k * tok:(k + 1) * tok].reshape(heads, piece, HEAD_SIZE)
                out_send[chunk, side * heads:(side + 1) * heads, :, k * HEAD_SIZE:(k + 1) * HEAD_SIZE] = block
                here = lax.rem(lane, group) == chunk * per_chunk + k
                lse[side] = jnp.where(here, level[k * tok:(k + 1) * tok], lse[side])
        spread(out_send.at[chunk], out_recv.at[chunk], chunk)
        return 0

    lse[...] = jnp.zeros_like(lse)
    lax.fori_loop(0, CHUNKS, chunk_step, 0)

    for side in range(2):
        level = lse[side]
        high = level.astype(jnp.bfloat16).astype(jnp.float32)
        middle = (level - high).astype(jnp.bfloat16).astype(jnp.float32)
        low = level - high - middle
        packed = jnp.where(lane < group, high, jnp.where(lane < 2 * group, middle, low)).astype(jnp.bfloat16)
        stat_send[side * heads:(side + 1) * heads] = packed.reshape(heads, piece, HEAD_SIZE)
    spread(stat_send, stat_recv, CHUNKS)

    for g in range(2):

        @pl.when(core != plane)
        def _():
            exchange(g).wait_send()

        for slot in range(nz):
            share(slot, g).wait_send()
        for d in range(1, last):
            for way in range(2):
                ring(way, d, g).wait_send()
        ring(0, last, g).wait_send()
    for r in range(2):
        for way in range(2):
            first(way, r).wait_send()
            second(way, r).wait_send()

    pltpu.make_async_copy(stat_send, stat_recv, o_recv.at[CHUNKS]).wait()
    for chunk in range(CHUNKS):
        pltpu.make_async_copy(out_send.at[chunk], out_recv.at[chunk], o_recv.at[chunk]).wait()

    for source in range(heads):
        levels = []
        for side in range(2):
            packed = stat_recv[side * heads + source].astype(jnp.float32)
            levels.append(
                packed + pltpu.roll(packed, HEAD_SIZE - group, 1) + pltpu.roll(packed, HEAD_SIZE - 2 * group, 1)
            )
        share_0 = 1.0 / (1.0 + jnp.exp2(levels[1] - levels[0]))
        for head in range(group):
            chunk, k = head // per_chunk, head % per_chunk
            columns = slice(k * HEAD_SIZE, (k + 1) * HEAD_SIZE)
            part_0 = out_recv[chunk, source, :, columns].astype(jnp.float32)
            part_1 = out_recv[chunk, heads + source, :, columns].astype(jnp.float32)
            portion = jnp.broadcast_to(share_0[:, head:head + 1], (piece, HEAD_SIZE))
            start = (source * group + head) * HEAD_SIZE
            out_ref[:, start:start + HEAD_SIZE] = (part_1 + portion * (part_0 - part_1)).astype(jnp.bfloat16)

    others = pl.ds(0, 2 * heads - 1)
    pltpu.make_async_copy(stat_send.at[others], stat_recv.at[others], o_send.at[CHUNKS]).wait()
    for chunk in range(CHUNKS):
        pltpu.make_async_copy(out_send.at[chunk, others], out_recv.at[chunk, others], o_send.at[chunk]).wait()


def solution(mesh):
    nz, heads = mesh.shape["seq"] // 4, mesh.shape["head"]

    def per_device(queries, keys, values, layout):
        tok, width = queries.shape
        group = width // HEAD_SIZE
        rows, piece = group // CHUNKS * tok, tok // heads
        tiles = nz // TILE + 1
        bf16, dma = jnp.bfloat16, pltpu.SemaphoreType.DMA
        vmem = pl.BlockSpec(memory_space=pltpu.VMEM)

        def body(*refs):
            kernel(nz, heads, *refs)

        return pl.pallas_call(
            body,
            out_shape=jax.ShapeDtypeStruct((piece, heads * width), bf16),
            in_specs=[pl.BlockSpec(memory_space=pltpu.SMEM), vmem, vmem, vmem],
            out_specs=vmem,
            scratch_shapes=[
                pltpu.VMEM((nz, 2, 2, tok, HEAD_SIZE), bf16),
                pltpu.VMEM((tok, width), bf16),
                pltpu.VMEM((2, 2, tok // 2, width // 2), bf16),
                pltpu.VMEM((2, CHUNKS, rows, HEAD_SIZE), bf16),
                pltpu.VMEM((tiles + 2, CHUNKS, rows, HEAD_SIZE), jnp.float32),
                pltpu.VMEM((tiles + 2, CHUNKS, rows, 2 * HEAD_SIZE), jnp.float32),
                pltpu.VMEM((CHUNKS, 2 * heads, piece, width // CHUNKS), bf16),
                pltpu.VMEM((CHUNKS, 2 * heads, piece, width // CHUNKS), bf16),
                pltpu.VMEM((2 * heads, piece, HEAD_SIZE), bf16),
                pltpu.VMEM((2 * heads, piece, HEAD_SIZE), bf16),
                pltpu.VMEM((2, tok, HEAD_SIZE), jnp.float32),
                pltpu.SMEM((tiles * TILE,), jnp.int32),
                pltpu.SMEM((tiles * TILE,), jnp.int32),
                pltpu.SMEM((3, nz), jnp.int32),
                dma((nz, 2)), dma((nz, 2)), dma((nz, 2)), dma((nz, 2)),
                dma((2,)), dma((2,)),
                dma((2, 2)), dma((2, 2)), dma((2, 2)), dma((2, 2)),
                dma((CHUNKS + 1,)), dma((CHUNKS + 1,)),
            ],
            compiler_params=pltpu.CompilerParams(
                collective_id=0, has_side_effects=True, vmem_limit_bytes=48 * 1024 * 1024
            ),
            cost_estimate=pl.CostEstimate(
                flops=4 * 2 * (nz + 1) * tok * group * tok * HEAD_SIZE,
                bytes_accessed=4 * tok * width,
                transcendentals=2 * (nz + 1) * tok * group * tok,
            ),
        )(layout, queries, keys, values)

    return jax.shard_map(
        per_device,
        mesh=mesh,
        in_specs=(P("seq", "head"), P("seq", "head"), P("seq", "head"), P()),
        out_specs=P(("seq", "head"), None),
        check_vma=False,
    )
```

time: 738 us -> 66.1 us (0.09); the launches traced: 725 us -> 65.8 us
  waiting for transfers between devices: 319 us -> 0 us
  starting transfers between devices: 245 us -> 0 us
  Pallas kernels: 0 us -> 62 us
  other arithmetic: 56 us -> 0 us
  loops' own time: 47.5 us -> 0 us
  matrix products: 42.6 us -> 0 us
  blocking collectives: 9.98 us -> 0 us
    ppermute x126 -> x0, waiting for transfers between devices: 319 us -> none  [passed_along(): return lax.ppermute(block, axis, route)]
    ppermute x126 -> x0, starting transfers between devices: 245 us -> none  [passed_along(): return lax.ppermute(block, axis, route)]
    pallas_call x0 -> x1, Pallas kernels: none -> 62 us  [per_device(): pl.pallas_call(body, out_shape=jax.ShapeDtypeStruct((piece, heads * width...]
    reduce_sum x128 -> x0, other arithmetic: 48.9 us -> none  [the longest x64 42.1 us: lookup(): return jnp.sum(jnp.where(slots == index, layout, 0))]
    another operation x1 -> x0, loops' own time: 47.5 us -> none  [per_device(): lax.fori_loop(1, seq_count, one_step, (carries, (keys, values)))]
    dot_general x128 -> x0, matrix products: 42.6 us -> none  [the longest x64 27.5 us: attend(): jnp.einsum('cgqk,kcd->cgqd', weight.astype(jnp.bfloat16), value_heads, pr...]
    all_to_all x1 -> x0, blocking collectives: 9.98 us -> none  [per_device(): lax.all_to_all(mixed, 'head', split_axis=0, concat_axis=1, tiled=True)]
  transfers between devices with their start and end apart: 126 -> 0, of which waited for: 126 -> 0; matrix products, arithmetic and copies ran while one was open for 10% -> 0% of each run, Pallas kernels for 0% -> 0%
where the time goes in v1:
time: 66.1 us; the launch traced here: 65.8 us
  Pallas kernels  62 us (94%)
  local copies, waits for them, and re-layouts  3.82 us (6%)
    pallas_call x1, Pallas kernels, per_device(): pl.pallas_call(body, out_shape=jax.ShapeDtypeStruct((piece, heads * width...  62 us
    unnamed x9, local copies, waits for them, and re-layouts  3.82 us

profile of v1, /device:TPU:1, one launch (start us, length us, event | category | flops | bytes accessed | tf_op | source)
XLA Modules:
  0.0 65.8 jit_solution(1145243314468108115)
XLA Ops:
  0.0 0.0 copy-start
  0.0 0.9 %copy-done = bf16[128,1024]{1,0:T(8,128)(2,1)S(1)} copy-done((bf16[128,1024]{1,0:T(8,128)(2,1)S(1)}, bf16[128,1024]{1,0:T(8,128)(2,1)}, u32[]{:S(2)}) %copy-start) | copy-done | bytes 262168
  1.0 0.0 copy-start.1
  1.0 0.8 %copy-done.1 = bf16[128,128]{1,0:T(8,128)(2,1)S(1)} copy-done((bf16[128,128]{1,0:T(8,128)(2,1)S(1)}, bf16[128,128]{1,0:T(8,128)(2,1)}, u32[]{:S(2)}) %copy-start.1) | copy-done | bytes 32792
  1.7 0.0 copy-start.2
  1.7 0.8 %copy-done.2 = bf16[128,128]{1,0:T(8,128)(2,1)S(1)} copy-done((bf16[128,128]{1,0:T(8,128)(2,1)S(1)}, bf16[128,128]{1,0:T(8,128)(2,1)}, u32[]{:S(2)}) %copy-start.2) | copy-done | bytes 32792
  2.5 0.0 copy-start.3
  2.5 0.7 copy-done.3
  3.1 62.0 %shard_map.46 = bf16[16,8192]{1,0:T(8,128)(2,1)S(1)} custom-call(s32[64]{0:T(128)S(1)} %copy-done.3, bf16[128,1024]{1,0:T(8,128)(2,1)S(1)} %copy-done, bf16[128,128]{1,0:T(8,128)(2,1)S(1)} %copy-done.1, bf16[128,128]{1,0:T(8,128)(2,1)S(1)} %copy-done.2), custom_call_target="tpu_custom_call" | custom-call | flops 2281701376 | bytes 524288 | tf_op jit(solution)/shard_map/pallas_call | solution.py:336
  65.1 0.7 %copy.6 = bf16[16,8192]{1,0:T(8,128)(2,1)} copy(bf16[16,8192]{1,0:T(8,128)(2,1)S(1)} %shard_map.46) | data formatting | bytes 524288
Async XLA Ops:
  0.0 0.9 %copy-start = (bf16[128,1024]{1,0:T(8,128)(2,1)S(1)}, bf16[128,1024]{1,0:T(8,128)(2,1)}, u32[]{:S(2)}) copy-start(bf16[128,1024]{1,0:T(8,128)(2,1)} %refs_1_.1) | copy-start | bytes 786436
  1.0 0.8 %copy-start.1 = (bf16[128,128]{1,0:T(8,128)(2,1)S(1)}, bf16[128,128]{1,0:T(8,128)(2,1)}, u32[]{:S(2)}) copy-start(bf16[128,128]{1,0:T(8,128)(2,1)} %refs_2_.1) | copy-start | bytes 98308
  1.7 0.8 %copy-start.2 = (bf16[128,128]{1,0:T(8,128)(2,1)S(1)}, bf16[128,128]{1,0:T(8,128)(2,1)}, u32[]{:S(2)}) copy-start(bf16[128,128]{1,0:T(8,128)(2,1)} %refs_3_.1) | copy-start | bytes 98308
  2.5 0.7 copy-start.3

commit v2 on v1

v2 whole, which is shorter than its diff:
```python
import math

import jax
import jax.numpy as jnp
from jax import lax
from jax.experimental import pallas as pl
from jax.experimental.pallas import tpu as pltpu
from jax.sharding import PartitionSpec as P


HEAD_SIZE = 128
MESH = pl.DeviceIdType.MESH
EMPTY = -1e30
SCALE = math.log2(math.e) / math.sqrt(HEAD_SIZE)
CHUNKS = 2
TILE = 4


def places(nz, heads):
    seq, h = lax.axis_index("seq"), lax.axis_index("head")
    return seq // (2 * nz), (seq // 2) % nz, seq % 2, h


def send(src, dst, send_sem, recv_sem, device):
    return pltpu.make_async_remote_copy(
        src_ref=src, dst_ref=dst, send_sem=send_sem, recv_sem=recv_sem, device_id=device, device_id_type=MESH
    )


def kernel(
    nz, heads, groups, layout_hbm, q_hbm, k_ref, v_ref, out_ref,
    kv_0, kv_1, kv_2, q_ref, qx, relay, qs, m_s, al_s, out_send, out_recv, stat_send, stat_recv, lse,
    layout_ref, pick, limit, place,
    ring_send, ring_recv, share_send, share_recv, cross_send, cross_recv,
    first_send, first_recv, second_send, second_recv, o_send, o_recv, local,
):
    tok, width = q_ref.shape
    group = width // HEAD_SIZE
    per_chunk = group // CHUNKS
    piece = tok // heads
    plane, z, core, h = places(nz, heads)
    nx = heads // 2
    y_lo, x = h // nx, h % nx
    last = nz // 2

    def at(p, zz, cc):
        return (p * nz + zz) * 2 + cc

    right, left = (at(plane, (z + 1) % nz, core), h), (at(plane, (z + nz - 1) % nz, core), h)
    sibling, cross = (at(plane, z, 1 - core), h), (at(1 - plane, z, 1 - core), h)
    above = (at((plane + y_lo) % 2, z, core), (1 - y_lo) * nx + x)
    below = (at((plane + 1 - y_lo) % 2, z, core), (1 - y_lo) * nx + x)

    def outward(e):
        return (plane + e // heads) % 2, (h + e % heads) % heads

    def device(e):
        p, j = outward(e)
        return at(p, z, core), j

    where = {slot: (buffer, n) for buffer, slots in zip((kv_0, kv_1, kv_2), groups) for n, slot in enumerate(slots)}

    def block(slot, whose, g=None):
        buffer, n = where[slot]
        return buffer.at[n, whose] if g is None else buffer.at[n, whose, g]

    def own(g):
        return pltpu.make_async_copy((k_ref, v_ref)[g], block(0, core, g), local.at[g])

    loads = (
        pltpu.make_async_copy(q_hbm, q_ref, local.at[2]),
        pltpu.make_async_copy(layout_hbm, layout_ref, local.at[3]),
    )

    @pl.when(core == plane)
    def _():
        for g in range(2):
            own(g).start()

    for load in loads:
        load.start()

    barrier = pltpu.get_barrier_semaphore()
    around = [right, left, sibling, cross] + [device(e) for e in range(1, 2 * heads)]
    for to in around:
        pl.semaphore_signal(barrier, inc=1, device_id=to, device_id_type=MESH)
    pl.semaphore_wait(barrier, len(around))

    def ring(way, d, g):
        src, dst, to = (d - 1, d, right) if way == 0 else ((nz - d + 1) % nz, nz - d, left)
        return send(block(src, core, g), block(dst, core, g), ring_send.at[dst, g], ring_recv.at[dst, g], to)

    def share(slot, whose):
        ref = block(slot, whose)
        return send(ref, ref, share_send.at[slot], share_recv.at[slot], sibling)

    def cross_copy(g, whose):
        return send((k_ref, v_ref)[g], block(0, whose, g), cross_send.at[g], cross_recv.at[g], cross)

    half, strip = width // 2, tok // 2

    def first(way, r):
        src = q_hbm.at[pl.ds(r * strip, strip), pl.ds(way * half, half)]
        return send(src, relay.at[way, r], first_send.at[way, r], first_recv.at[way, r], (above, below)[way])

    def second(way, r):
        dst = qx.at[pl.ds(r * strip, strip), pl.ds(way * half, half)]
        return send(relay.at[way, r], dst, second_send.at[way, r], second_recv.at[way, r], (above, below)[way])

    @pl.when(core != plane)
    def _():
        for g in range(2):
            cross_copy(g, 1 - core).start()

    for g in range(2):

        @pl.when(core != plane)
        def _():
            cross_copy(g, core).wait_recv()

        @pl.when(core == plane)
        def _():
            own(g).wait()

        for way in range(2):
            ring(way, 1, g).start()
    share(0, core).start()
    for r in range(2):
        for way in range(2):
            first(way, r).start()
    for load in loads:
        load.wait()

    own_block = layout_ref[2 * z + core]
    low_tiles, starts, tile_counts = [], [], []
    start = 0
    for slots in groups:
        tiles = len(slots) // TILE + 1
        positions = [layout_ref[2 * ((z + nz - slot) % nz) + plane] for slot in slots]
        count = jnp.int32(0)
        for position in positions:
            count += (position <= own_block).astype(jnp.int32)
        low = (count + TILE - 1) // TILE
        low_next, high_next = jnp.int32(0), low * TILE
        for n, position in enumerate(positions):
            is_low, is_high = position <= own_block, position >= own_block
            place[0, n] = jnp.where(is_low, low_next, -1)
            place[1, n] = jnp.where(is_high, high_next, -1)
            place[2, n] = jnp.where(position == own_block, 0, tok)
            low_next += is_low.astype(jnp.int32)
            high_next += is_high.astype(jnp.int32)

        def order(t, _):
            index, bound = jnp.int32(0), jnp.int32(-tok)
            for n in range(len(slots)):
                here = (place[0, n] == t) | (place[1, n] == t)
                index = jnp.where(here, n, index)
                bound = jnp.where(here, place[2, n], bound)
            pick[start + t] = index
            limit[start + t] = bound
            return 0

        lax.fori_loop(0, tiles * TILE, order, 0)
        low_tiles.append(low)
        starts.append(start)
        tile_counts.append(tiles)
        start += tiles * TILE

    def scaled(target, ref):
        for head in range(group):
            part = ref[:, head * HEAD_SIZE:(head + 1) * HEAD_SIZE].astype(jnp.float32) * SCALE
            qs[target, head] = part.astype(jnp.bfloat16)

    scaled(plane, q_ref)
    ones = jnp.ones((TILE * tok, HEAD_SIZE), jnp.bfloat16)

    def tile(side, keys, values, before, after, bounds, offset, count):
        values = jnp.concatenate([values, ones], axis=1)

        def scores(n):
            return lax.dot_general(
                qs[side, offset + n], keys, (((1,), (1,)), ((), ())), preferred_element_type=jnp.float32
            )

        if bounds is not None:
            ahead = lax.broadcasted_iota(jnp.int32, (tok, tok), 1) - lax.broadcasted_iota(jnp.int32, (tok, tok), 0)
        upcoming = scores(0)
        for n in range(count):
            score = upcoming
            if n + 1 < count:
                upcoming = scores(n + 1)
            parts = [score[:, j * tok:(j + 1) * tok] for j in range(TILE)]
            if bounds is not None:
                parts = [jnp.where(ahead <= bounds[j], parts[j], EMPTY) for j in range(TILE)]
            widest = parts[0]
            for part in parts[1:]:
                widest = jnp.maximum(widest, part)
            top = jnp.max(widest, axis=1, keepdims=True)
            if before is None:
                m_next = jnp.broadcast_to(top, (tok, HEAD_SIZE))
            else:
                m = m_s[before, offset + n]
                m_next = jnp.maximum(m, top)
            weight = jnp.concatenate([jnp.exp2(part - m_next).astype(jnp.bfloat16) for part in parts], axis=1)
            mixed = jnp.dot(weight, values, preferred_element_type=jnp.float32)
            if before is not None:
                factor = jnp.exp2(m - m_next)
                mixed += al_s[before, offset + n] * jnp.concatenate([factor, factor], axis=1)
            m_s[after, offset + n] = m_next
            al_s[after, offset + n] = mixed

    m_s[0] = jnp.full(m_s.shape[1:], EMPTY, jnp.float32)
    al_s[0] = jnp.zeros(al_s.shape[1:], jnp.float32)

    def first_part(slots, before, after, offset, count):
        keys = jnp.concatenate([block(slot, 0, 0)[...] for slot in slots], axis=0)
        values = jnp.concatenate([block(slot, 0, 1)[...] for slot in slots], axis=0)
        tile(1, keys, values, before, after, None, offset, count)

    def second_part(index, low_before, high_before, after, offset, count):
        buffer, low, begin = (kv_0, kv_1, kv_2)[index], low_tiles[index], starts[index]

        def step(t, _):
            side = jnp.where(t < low, 0, 1)
            before = jnp.where(t == low, high_before, jnp.where(t == 0, low_before, after + t - 1))
            chosen = [pick[begin + t * TILE + j] for j in range(TILE)]
            bounds = [limit[begin + t * TILE + j] for j in range(TILE)]
            keys = jnp.concatenate([buffer[n, side, 0] for n in chosen], axis=0)
            values = jnp.concatenate([buffer[n, side, 1] for n in chosen], axis=0)
            tile(side, keys, values, before, after + t, bounds, offset, count)
            return 0

        lax.fori_loop(0, tile_counts[index], step, 0)
        return jnp.where(low == 0, low_before, after + low - 1), after + tile_counts[index] - 1

    def arrived(slots):
        for slot in slots:
            share(slot, 1 - core).wait_recv()

    near, middle, far = groups
    low_at, high_at = 0, None
    for d in range(1, last + 1):
        for g in range(2):
            if d < last:
                for way in range(2):
                    ring(way, d, g).wait_recv()
                    if d + 1 < last:
                        ring(way, d + 1, g).start()
                    else:

                        @pl.when(core == way)
                        def _():
                            ring(way, d + 1, g).start()
            else:
                ring(0, d, g).wait_recv()
        share(d, core).start()
        if d < last:
            share(nz - d, core).start()
        if d <= 2:
            for way in range(2):
                first(way, d - 1).wait_recv()
                second(way, d - 1).start()
        if d == 3:
            for r in range(2):
                for way in range(2):
                    second(way, r).wait_recv()
            scaled(1 - plane, qx)
            arrived(near[:TILE])
            first_part(near[:TILE], None, 1, 0, group)
        if d == 5:
            arrived(near[TILE:])
            first_part(near[TILE:], 1, 2, 0, group)
        if d == last - 1:
            low_at, high_at = second_part(0, 0, 2, 3, 0, group)
            arrived(middle)
            first_part(middle, high_at, high_at + 1, 0, group)
            low_at, high_at = second_part(1, low_at, high_at + 1, high_at + 2, 0, group)
    arrived(far)

    lane = lax.broadcasted_iota(jnp.int32, (tok, HEAD_SIZE), 1)
    mine = plane * heads + h
    far_first = sorted(range(1, 2 * heads), key=lambda e: (e % heads) not in (0, 2, 6))

    def spread(buffer, landing, index):
        for e in far_first:
            p, j = outward(e)
            send(
                buffer.at[p * heads + j], landing.at[mine], o_send.at[index], o_recv.at[index], device(e)
            ).start()
        pltpu.make_async_copy(buffer.at[mine], landing.at[mine], o_recv.at[index]).start()

    lse[...] = jnp.zeros_like(lse)

    def chunk_step(chunk, _):
        offset = chunk * per_chunk
        first_part(far, high_at, high_at + 1, offset, per_chunk)
        ends = second_part(2, low_at, high_at + 1, high_at + 2, offset, per_chunk)
        for side in range(2):
            for n in range(per_chunk):
                m, al = m_s[ends[side], offset + n], al_s[ends[side], offset + n]
                total = al[:, HEAD_SIZE:]
                some = total > 0.0
                safe = jnp.where(some, total, 1.0)
                mixed = (al[:, :HEAD_SIZE] / safe).astype(jnp.bfloat16)
                out_send[chunk, side * heads:(side + 1) * heads, :, n * HEAD_SIZE:(n + 1) * HEAD_SIZE] = (
                    mixed.reshape(heads, piece, HEAD_SIZE)
                )
                level = jnp.where(some, m + jnp.log2(safe), EMPTY)
                lse[side] = jnp.where(lax.rem(lane, group) == offset + n, level, lse[side])
        spread(out_send.at[chunk], out_recv.at[chunk], chunk)
        return 0

    lax.fori_loop(0, CHUNKS, chunk_step, 0)

    for side in range(2):
        level = lse[side]
        high = level.astype(jnp.bfloat16).astype(jnp.float32)
        rest = (level - high).astype(jnp.bfloat16).astype(jnp.float32)
        low = level - high - rest
        packed = jnp.where(lane < group, high, jnp.where(lane < 2 * group, rest, low)).astype(jnp.bfloat16)
        stat_send[side * heads:(side + 1) * heads] = packed.reshape(heads, piece, HEAD_SIZE)
    spread(stat_send, stat_recv, CHUNKS)

    for slot in range(nz):
        share(slot, core).wait_send()
    for g in range(2):

        @pl.when(core != plane)
        def _():
            cross_copy(g, 1 - core).wait_send()

        for d in range(1, last):
            for way in range(2):
                ring(way, d, g).wait_send()
        ring(0, last, g).wait_send()
    for r in range(2):
        for way in range(2):
            first(way, r).wait_send()
            second(way, r).wait_send()

    pltpu.make_async_copy(stat_send, stat_recv, o_recv.at[CHUNKS]).wait()
    for chunk in range(CHUNKS):
        pltpu.make_async_copy(out_send.at[chunk], out_recv.at[chunk], o_recv.at[chunk]).wait()

    for source in range(heads):
        levels = []
        for side in range(2):
            packed = stat_recv[side * heads + source].astype(jnp.float32)
            levels.append(
                packed + pltpu.roll(packed, HEAD_SIZE - group, 1) + pltpu.roll(packed, HEAD_SIZE - 2 * group, 1)
            )
        share_0 = 1.0 / (1.0 + jnp.exp2(levels[1] - levels[0]))
        for head in range(group):
            chunk, n = head // per_chunk, head % per_chunk
            columns = slice(n * HEAD_SIZE, (n + 1) * HEAD_SIZE)
            part_0 = out_recv[chunk, source, :, columns].astype(jnp.float32)
            part_1 = out_recv[chunk, heads + source, :, columns].astype(jnp.float32)
            portion = jnp.broadcast_to(share_0[:, head:head + 1], (piece, HEAD_SIZE))
            start = (source * group + head) * HEAD_SIZE
            out_ref[:, start:start + HEAD_SIZE] = (part_1 + portion * (part_0 - part_1)).astype(jnp.bfloat16)

    others = pl.ds(0, 2 * heads - 1)
    pltpu.make_async_copy(stat_send.at[others], stat_recv.at[others], o_send.at[CHUNKS]).wait()
    for chunk in range(CHUNKS):
        pltpu.make_async_copy(out_send.at[chunk, others], out_recv.at[chunk, others], o_send.at[chunk]).wait()


def solution(mesh):
    nz, heads = mesh.shape["seq"] // 4, mesh.shape["head"]
    arrival = [0] + [slot for d in range(1, nz // 2) for slot in (d, nz - d)] + [nz // 2]
    groups = (arrival[:2 * TILE], arrival[2 * TILE:3 * TILE], arrival[3 * TILE:])

    def per_device(queries, keys, values, layout):
        tok, width = queries.shape
        group = width // HEAD_SIZE
        piece = tok // heads
        entries = sum(len(slots) // TILE + 1 for slots in groups) * TILE
        states = 1 + nz // TILE + entries // TILE
        bf16, f32, dma = jnp.bfloat16, jnp.float32, pltpu.SemaphoreType.DMA
        anywhere = pl.BlockSpec(memory_space=pl.ANY)

        return pl.pallas_call(
            lambda *refs: kernel(nz, heads, groups, *refs),
            out_shape=jax.ShapeDtypeStruct((piece, heads * width), bf16),
            in_specs=[anywhere] * 4,
            out_specs=pl.BlockSpec(memory_space=pltpu.VMEM),
            scratch_shapes=[pltpu.VMEM((len(slots), 2, 2, tok, HEAD_SIZE), bf16) for slots in groups]
            + [
                pltpu.VMEM((tok, width), bf16),
                pltpu.VMEM((tok, width), bf16),
                pltpu.VMEM((2, 2, tok // 2, width // 2), bf16),
                pltpu.VMEM((2, group, tok, HEAD_SIZE), bf16),
                pltpu.VMEM((states, group, tok, HEAD_SIZE), f32),
                pltpu.VMEM((states, group, tok, 2 * HEAD_SIZE), f32),
                pltpu.VMEM((CHUNKS, 2 * heads, piece, width // CHUNKS), bf16),
                pltpu.VMEM((CHUNKS, 2 * heads, piece, width // CHUNKS), bf16),
                pltpu.VMEM((2 * heads, piece, HEAD_SIZE), bf16),
                pltpu.VMEM((2 * heads, piece, HEAD_SIZE), bf16),
                pltpu.VMEM((2, tok, HEAD_SIZE), f32),
                pltpu.SMEM(layout.shape, jnp.int32),
                pltpu.SMEM((entries,), jnp.int32),
                pltpu.SMEM((entries,), jnp.int32),
                pltpu.SMEM((3, 2 * TILE), jnp.int32),
                dma((nz, 2)), dma((nz, 2)), dma((nz,)), dma((nz,)), dma((2,)), dma((2,)),
                dma((2, 2)), dma((2, 2)), dma((2, 2)), dma((2, 2)),
                dma((CHUNKS + 1,)), dma((CHUNKS + 1,)), dma((4,)),
            ],
            compiler_params=pltpu.CompilerParams(
                collective_id=0, has_side_effects=True, vmem_limit_bytes=60 * 1024 * 1024
            ),
            cost_estimate=pl.CostEstimate(
                flops=4 * 2 * (nz + 1) * tok * group * tok * HEAD_SIZE,
                bytes_accessed=4 * tok * width,
                transcendentals=2 * (nz + 1) * tok * group * tok,
            ),
        )(layout, queries, keys, values)

    return jax.shard_map(
        per_device,
        mesh=mesh,
        in_specs=(P("seq", "head"), P("seq", "head"), P("seq", "head"), P()),
        out_specs=P(("seq", "head"), None),
        check_vma=False,
    )
```

time: 66.1 us -> 64.7 us (0.979)
  local copies, waits for them, and re-layouts: 3.82 us -> 1.67 us
  Pallas kernels: 62 us -> 62.9 us
    unnamed x9 -> x1, local copies, waits for them, and re-layouts: 3.82 us -> 1.67 us
    pallas_call x1, Pallas kernels: 62 us -> 62.9 us  [per_device(): pl.pallas_call(lambda *refs: kernel(nz, heads, groups, *refs), out_shape=...]
where the time goes in v2:
time: 64.7 us; the launch traced here: 64.6 us
  Pallas kernels  62.9 us (97%)
  local copies, waits for them, and re-layouts  1.67 us (3%)
    pallas_call x1, Pallas kernels, per_device(): pl.pallas_call(lambda *refs: kernel(nz, heads, groups, *refs), out_shape=...  62.9 us
    unnamed x1, local copies, waits for them, and re-layouts  1.67 us

profile of v2, /device:TPU:1, one launch (start us, length us, event | category | flops | bytes accessed | tf_op | source)
XLA Modules:
  0.0 64.6 jit_solution(10510494348696543918)
XLA Ops:
  0.0 62.9 %shard_map.46 = bf16[16,8192]{1,0:T(8,128)(2,1)} custom-call(s32[64]{0:T(128)} %refs_0_.1, bf16[128,1024]{1,0:T(8,128)(2,1)} %refs_1_.1, bf16[128,128]{1,0:T(8,128)(2,1)} %refs_2_.1, bf16[128,128]{1,0:T(8,128)(2,1)} %refs_3_.1), custom_call_target="tpu_custom_call" | custom-call | flops 2281701376 | bytes 524288 | tf_op jit(solution)/shard_map/pallas_call | solution.py:382
  62.9 1.7 %copy.6 = bf16[16,8192]{1,0:T(8,128)(2,1)} copy(bf16[16,8192]{1,0:T(8,128)(2,1)} %shard_map.46) | data formatting | bytes 524288

commit v3 on v2

--- a/solution.py
+++ b/solution.py
@@ -16,6 +16,10 @@
 TILE = 4
 
 
+def tiles_for(slots):
+    return (len(slots) + (0 in slots) - 2) // TILE + 2
+
+
 def places(nz, heads):
     seq, h = lax.axis_index("seq"), lax.axis_index("head")
     return seq // (2 * nz), (seq // 2) % nz, seq % 2, h
@@ -28,7 +32,7 @@
 
 
 def kernel(
-    nz, heads, groups, layout_hbm, q_hbm, k_ref, v_ref, out_ref,
+    nz, heads, arrival, groups, layout_hbm, q_hbm, k_ref, v_ref, out_ref,
     kv_0, kv_1, kv_2, q_ref, qx, relay, qs, m_s, al_s, out_send, out_recv, stat_send, stat_recv, lse,
     layout_ref, pick, limit, place,
     ring_send, ring_recv, share_send, share_recv, cross_send, cross_recv,
@@ -46,8 +50,10 @@
     def at(p, zz, cc):
         return (p * nz + zz) * 2 + cc
 
-    right, left = (at(plane, (z + 1) % nz, core), h), (at(plane, (z + nz - 1) % nz, core), h)
-    sibling, cross = (at(plane, z, 1 - core), h), (at(1 - plane, z, 1 - core), h)
+    step_to = jnp.where(core == 0, 1, nz - 1)
+    onward, backward = (at(plane, (z + step_to) % nz, core), h), (at(plane, (z + nz - step_to) % nz, core), h)
+    sibling = (at(plane, z, 1 - core), h)
+    opposite = [(at(1 - plane, z, cc), h) for cc in range(2)]
     above = (at((plane + y_lo) % 2, z, core), (1 - y_lo) * nx + x)
     below = (at((plane + 1 - y_lo) % 2, z, core), (1 - y_lo) * nx + x)
 
@@ -58,14 +64,32 @@
         p, j = outward(e)
         return at(p, z, core), j
 
-    where = {slot: (buffer, n) for buffer, slots in zip((kv_0, kv_1, kv_2), groups) for n, slot in enumerate(slots)}
-
-    def block(slot, whose, g=None):
+    buffers = (kv_0, kv_1, kv_2)
+
+    def spot(d, whose):
+        if d == 0:
+            return kv_0, 0
+        if d == last:
+            return kv_2, len(groups[2]) - 1
+        index = 2 * d - 1 + whose
+        for buffer, slots, begin in zip(buffers, groups, (0, len(groups[0]), len(groups[0]) + len(groups[1]))):
+            if begin <= 2 * d - 1 < begin + len(slots):
+                return buffer, index - begin
+
+    where = {slot: (buffer, n) for buffer, slots in zip(buffers, groups) for n, slot in enumerate(slots)}
+
+    def block(slot, whose, g):
         buffer, n = where[slot]
-        return buffer.at[n, whose] if g is None else buffer.at[n, whose, g]
+        return buffer.at[n, whose, g]
+
+    sides = (plane, 1 - plane)
+
+    def granule(d, b, g):
+        buffer, n = spot(d, core)
+        return buffer.at[n, sides[b], g]
 
     def own(g):
-        return pltpu.make_async_copy((k_ref, v_ref)[g], block(0, core, g), local.at[g])
+        return pltpu.make_async_copy((k_ref, v_ref)[g], granule(0, 0, g), local.at[g])
 
     loads = (
         pltpu.make_async_copy(q_hbm, q_ref, local.at[2]),
@@ -81,21 +105,31 @@
         load.start()
 
     barrier = pltpu.get_barrier_semaphore()
-    around = [right, left, sibling, cross] + [device(e) for e in range(1, 2 * heads)]
+    around = [onward, backward, sibling, (at(1 - plane, z, 1 - core), h)] + [device(e) for e in range(1, 2 * heads)]
     for to in around:
         pl.semaphore_signal(barrier, inc=1, device_id=to, device_id_type=MESH)
     pl.semaphore_wait(barrier, len(around))
 
-    def ring(way, d, g):
-        src, dst, to = (d - 1, d, right) if way == 0 else ((nz - d + 1) % nz, nz - d, left)
-        return send(block(src, core, g), block(dst, core, g), ring_send.at[dst, g], ring_recv.at[dst, g], to)
-
-    def share(slot, whose):
-        ref = block(slot, whose)
-        return send(ref, ref, share_send.at[slot], share_recv.at[slot], sibling)
-
-    def cross_copy(g, whose):
-        return send((k_ref, v_ref)[g], block(0, whose, g), cross_send.at[g], cross_recv.at[g], cross)
+    def ring(d, b, g):
+        return send(
+            granule(d - 1, b, g), granule(d, b, g), ring_send.at[d - 1, b, g], ring_recv.at[d - 1, b, g], onward
+        )
+
+    def share(d, whose):
+        buffer, n = spot(d, whose)
+        ref = buffer.at[n, jnp.where(whose == 0, plane, 1 - plane)] if d == last else buffer.at[n]
+        return send(ref, ref, share_send.at[d - 1], share_recv.at[d - 1], sibling)
+
+    def home(g):
+        return send((k_ref, v_ref)[g], granule(0, 0, g), cross_send.at[0, g], cross_recv.at[0, g], sibling)
+
+    def abroad(cc, g):
+        return send(
+            (k_ref, v_ref)[g], granule(0, 0, g), cross_send.at[cc, g], cross_recv.at[1, g], opposite[cc]
+        )
+
+    def from_abroad(g):
+        return send((k_ref, v_ref)[g], granule(0, 1, g), cross_send.at[1, g], cross_recv.at[1, g], opposite[0])
 
     half, strip = width // 2, tok // 2
 
@@ -110,24 +144,31 @@
     @pl.when(core != plane)
     def _():
         for g in range(2):
-            cross_copy(g, 1 - core).start()
+            for cc in range(2):
+                abroad(cc, g).start()
+
+    @pl.when(core == plane)
+    def _():
+        for g in range(2):
+            home(g).start()
 
     for g in range(2):
 
         @pl.when(core != plane)
         def _():
-            cross_copy(g, core).wait_recv()
+            home(g).wait_recv()
 
         @pl.when(core == plane)
         def _():
             own(g).wait()
 
-        for way in range(2):
-            ring(way, 1, g).start()
-    share(0, core).start()
+        ring(1, 0, g).start()
     for r in range(2):
         for way in range(2):
             first(way, r).start()
+    for g in range(2):
+        from_abroad(g).wait_recv()
+        ring(1, 1, g).start()
     for load in loads:
         load.wait()
 
@@ -135,7 +176,7 @@
     low_tiles, starts, tile_counts = [], [], []
     start = 0
     for slots in groups:
-        tiles = len(slots) // TILE + 1
+        tiles = tiles_for(slots)
         positions = [layout_ref[2 * ((z + nz - slot) % nz) + plane] for slot in slots]
         count = jnp.int32(0)
         for position in positions:
@@ -217,45 +258,51 @@
         values = jnp.concatenate([block(slot, 0, 1)[...] for slot in slots], axis=0)
         tile(1, keys, values, before, after, None, offset, count)
 
-    def second_part(index, low_before, high_before, after, offset, count):
-        buffer, low, begin = (kv_0, kv_1, kv_2)[index], low_tiles[index], starts[index]
+    def second_part(index, low_before, high_before, after, offset, count, begin=0, end=None):
+        buffer, low, base, tiles = buffers[index], low_tiles[index], starts[index], tile_counts[index]
 
         def step(t, _):
             side = jnp.where(t < low, 0, 1)
             before = jnp.where(t == low, high_before, jnp.where(t == 0, low_before, after + t - 1))
-            chosen = [pick[begin + t * TILE + j] for j in range(TILE)]
-            bounds = [limit[begin + t * TILE + j] for j in range(TILE)]
+            chosen = [pick[base + t * TILE + j] for j in range(TILE)]
+            bounds = [limit[base + t * TILE + j] for j in range(TILE)]
             keys = jnp.concatenate([buffer[n, side, 0] for n in chosen], axis=0)
             values = jnp.concatenate([buffer[n, side, 1] for n in chosen], axis=0)
             tile(side, keys, values, before, after + t, bounds, offset, count)
             return 0
 
-        lax.fori_loop(0, tile_counts[index], step, 0)
-        return jnp.where(low == 0, low_before, after + low - 1), after + tile_counts[index] - 1
-
-    def arrived(slots):
-        for slot in slots:
-            share(slot, 1 - core).wait_recv()
-
-    near, middle, far = groups
-    low_at, high_at = 0, None
+        lax.fori_loop(begin, tiles if end is None else end, step, 0)
+        return (
+            jnp.where(low == 0, low_before, after + low - 1),
+            jnp.where(low == tiles, high_before, after + tiles - 1),
+        )
+
+    def shared(*steps):
+        for d in steps:
+            share(d, 1 - core).wait_recv()
+
+    parts = [arrival[i:i + TILE] for i in range(0, nz, TILE)]
     for d in range(1, last + 1):
-        for g in range(2):
-            if d < last:
-                for way in range(2):
-                    ring(way, d, g).wait_recv()
-                    if d + 1 < last:
-                        ring(way, d + 1, g).start()
-                    else:
-
-                        @pl.when(core == way)
-                        def _():
-                            ring(way, d + 1, g).start()
+        for b in range(2):
+            if d < last - 1:
+                for g in range(2):
+                    ring(d, b, g).wait_recv()
+                    ring(d + 1, b, g).start()
+            elif d == last - 1:
+                for g in range(2):
+                    ring(d, b, g).wait_recv()
+
+                @pl.when(core == b)
+                def _():
+                    for g in range(2):
+                        ring(last, b, g).start()
             else:
-                ring(0, d, g).wait_recv()
+
+                @pl.when(core == b)
+                def _():
+                    for g in range(2):
+                        ring(last, b, g).wait_recv()
         share(d, core).start()
-        if d < last:
-            share(nz - d, core).start()
         if d <= 2:
             for way in range(2):
                 first(way, d - 1).wait_recv()
@@ -265,17 +312,21 @@
                 for way in range(2):
                     second(way, r).wait_recv()
             scaled(1 - plane, qx)
-            arrived(near[:TILE])
-            first_part(near[:TILE], None, 1, 0, group)
+            shared(1, 2)
+            first_part(parts[0], None, 1, 0, group)
+        if d == 4:
+            shared(3)
+            second_part(0, 0, 1, 3, 0, group, 0, 2)
         if d == 5:
-            arrived(near[TILE:])
-            first_part(near[TILE:], 1, 2, 0, group)
-        if d == last - 1:
-            low_at, high_at = second_part(0, 0, 2, 3, 0, group)
-            arrived(middle)
-            first_part(middle, high_at, high_at + 1, 0, group)
-            low_at, high_at = second_part(1, low_at, high_at + 1, high_at + 2, 0, group)
-    arrived(far)
+            low_at, high_at = second_part(0, 0, 1, 3, 0, group, 2, 3)
+        if d == 6:
+            shared(4)
+            first_part(parts[1], high_at, 2, 0, group)
+        if d == 7:
+            shared(5, 6)
+            first_part(parts[2], 2, 6, 0, group)
+            low_at, high_at = second_part(1, low_at, 6, 7, 0, group)
+    shared(last - 1, last)
 
     lane = lax.broadcasted_iota(jnp.int32, (tok, HEAD_SIZE), 1)
     mine = plane * heads + h
@@ -293,8 +344,8 @@
 
     def chunk_step(chunk, _):
         offset = chunk * per_chunk
-        first_part(far, high_at, high_at + 1, offset, per_chunk)
-        ends = second_part(2, low_at, high_at + 1, high_at + 2, offset, per_chunk)
+        first_part(parts[3], high_at, 9, offset, per_chunk)
+        ends = second_part(2, low_at, 9, 10, offset, per_chunk)
         for side in range(2):
             for n in range(per_chunk):
                 m, al = m_s[ends[side], offset + n], al_s[ends[side], offset + n]
@@ -321,18 +372,26 @@
         stat_send[side * heads:(side + 1) * heads] = packed.reshape(heads, piece, HEAD_SIZE)
     spread(stat_send, stat_recv, CHUNKS)
 
-    for slot in range(nz):
-        share(slot, core).wait_send()
+    for d in range(1, last + 1):
+        share(d, core).wait_send()
     for g in range(2):
 
         @pl.when(core != plane)
         def _():
-            cross_copy(g, 1 - core).wait_send()
-
-        for d in range(1, last):
-            for way in range(2):
-                ring(way, d, g).wait_send()
-        ring(0, last, g).wait_send()
+            for cc in range(2):
+                abroad(cc, g).wait_send()
+
+        @pl.when(core == plane)
+        def _():
+            home(g).wait_send()
+
+        for b in range(2):
+            for d in range(1, last):
+                ring(d, b, g).wait_send()
+
+            @pl.when(core == b)
+            def _():
+                ring(last, b, g).wait_send()
     for r in range(2):
         for way in range(2):
             first(way, r).wait_send()
@@ -368,19 +427,19 @@
 def solution(mesh):
     nz, heads = mesh.shape["seq"] // 4, mesh.shape["head"]
     arrival = [0] + [slot for d in range(1, nz // 2) for slot in (d, nz - d)] + [nz // 2]
-    groups = (arrival[:2 * TILE], arrival[2 * TILE:3 * TILE], arrival[3 * TILE:])
+    groups = (arrival[:2 * TILE - 1], arrival[2 * TILE - 1:3 * TILE - 1], arrival[3 * TILE - 1:])
 
     def per_device(queries, keys, values, layout):
         tok, width = queries.shape
         group = width // HEAD_SIZE
         piece = tok // heads
-        entries = sum(len(slots) // TILE + 1 for slots in groups) * TILE
+        entries = sum(tiles_for(slots) for slots in groups) * TILE
         states = 1 + nz // TILE + entries // TILE
         bf16, f32, dma = jnp.bfloat16, jnp.float32, pltpu.SemaphoreType.DMA
         anywhere = pl.BlockSpec(memory_space=pl.ANY)
 
         return pl.pallas_call(
-            lambda *refs: kernel(nz, heads, groups, *refs),
+            lambda *refs: kernel(nz, heads, arrival, groups, *refs),
             out_shape=jax.ShapeDtypeStruct((piece, heads * width), bf16),
             in_specs=[anywhere] * 4,
             out_specs=pl.BlockSpec(memory_space=pltpu.VMEM),
@@ -401,7 +460,7 @@
                 pltpu.SMEM((entries,), jnp.int32),
                 pltpu.SMEM((entries,), jnp.int32),
                 pltpu.SMEM((3, 2 * TILE), jnp.int32),
-                dma((nz, 2)), dma((nz, 2)), dma((nz,)), dma((nz,)), dma((2,)), dma((2,)),
+                dma((nz // 2, 2, 2)), dma((nz // 2, 2, 2)), dma((nz // 2,)), dma((nz // 2,)), dma((2, 2)), dma((2, 2)),
                 dma((2, 2)), dma((2, 2)), dma((2, 2)), dma((2, 2)),
                 dma((CHUNKS + 1,)), dma((CHUNKS + 1,)), dma((4,)),
             ],

time: 64.7 us -> 61.1 us (0.944)
  Pallas kernels: 62.9 us -> 59.3 us
    pallas_call x1, Pallas kernels: 62.9 us -> 59.3 us  [per_device(): pl.pallas_call(lambda *refs: kernel(nz, heads, arrival, groups, *refs), o...]
where the time goes in v3:
time: 61.1 us; the launch traced here: 61 us
  Pallas kernels  59.3 us (97%)
  local copies, waits for them, and re-layouts  1.67 us (3%)
    pallas_call x1, Pallas kernels, per_device(): pl.pallas_call(lambda *refs: kernel(nz, heads, arrival, groups, *refs), o...  59.3 us
    unnamed x1, local copies, waits for them, and re-layouts  1.67 us

profile of v3, /device:TPU:1, one launch (start us, length us, event | category | flops | bytes accessed | tf_op | source)
XLA Modules:
  0.0 61.0 jit_solution(10709633971977047362)
XLA Ops:
  0.0 59.3 %shard_map.46 = bf16[16,8192]{1,0:T(8,128)(2,1)} custom-call(s32[64]{0:T(128)} %refs_0_.1, bf16[128,1024]{1,0:T(8,128)(2,1)} %refs_1_.1, bf16[128,128]{1,0:T(8,128)(2,1)} %refs_2_.1, bf16[128,128]{1,0:T(8,128)(2,1)} %refs_3_.1), custom_call_target="tpu_custom_call" | custom-call | flops 2281701376 | bytes 524288 | tf_op jit(solution)/shard_map/pallas_call | solution.py:441
  59.3 1.7 %copy.6 = bf16[16,8192]{1,0:T(8,128)(2,1)} copy(bf16[16,8192]{1,0:T(8,128)(2,1)} %shard_map.46) | data formatting | bytes 524288

commit v4 on v3

--- a/solution.py
+++ b/solution.py
@@ -169,25 +169,22 @@
     for g in range(2):
         from_abroad(g).wait_recv()
         ring(1, 1, g).start()
-    for load in loads:
-        load.wait()
-
-    own_block = layout_ref[2 * z + core]
-    low_tiles, starts, tile_counts = [], [], []
-    start = 0
-    for slots in groups:
-        tiles = tiles_for(slots)
+
+    own_block, low_tiles, starts, tile_counts = [], [], [], []
+
+    def arrange(slots):
+        tiles, start = tiles_for(slots), sum(tile_counts) * TILE
         positions = [layout_ref[2 * ((z + nz - slot) % nz) + plane] for slot in slots]
         count = jnp.int32(0)
         for position in positions:
-            count += (position <= own_block).astype(jnp.int32)
+            count += (position <= own_block[0]).astype(jnp.int32)
         low = (count + TILE - 1) // TILE
         low_next, high_next = jnp.int32(0), low * TILE
         for n, position in enumerate(positions):
-            is_low, is_high = position <= own_block, position >= own_block
+            is_low, is_high = position <= own_block[0], position >= own_block[0]
             place[0, n] = jnp.where(is_low, low_next, -1)
             place[1, n] = jnp.where(is_high, high_next, -1)
-            place[2, n] = jnp.where(position == own_block, 0, tok)
+            place[2, n] = jnp.where(position == own_block[0], 0, tok)
             low_next += is_low.astype(jnp.int32)
             high_next += is_high.astype(jnp.int32)
 
@@ -205,14 +202,12 @@
         low_tiles.append(low)
         starts.append(start)
         tile_counts.append(tiles)
-        start += tiles * TILE
 
     def scaled(target, ref):
         for head in range(group):
             part = ref[:, head * HEAD_SIZE:(head + 1) * HEAD_SIZE].astype(jnp.float32) * SCALE
             qs[target, head] = part.astype(jnp.bfloat16)
 
-    scaled(plane, q_ref)
     ones = jnp.ones((TILE * tok, HEAD_SIZE), jnp.bfloat16)
 
     def tile(side, keys, values, before, after, bounds, offset, count):
@@ -250,9 +245,6 @@
             m_s[after, offset + n] = m_next
             al_s[after, offset + n] = mixed
 
-    m_s[0] = jnp.full(m_s.shape[1:], EMPTY, jnp.float32)
-    al_s[0] = jnp.zeros(al_s.shape[1:], jnp.float32)
-
     def first_part(slots, before, after, offset, count):
         keys = jnp.concatenate([block(slot, 0, 0)[...] for slot in slots], axis=0)
         values = jnp.concatenate([block(slot, 0, 1)[...] for slot in slots], axis=0)
@@ -271,7 +263,11 @@
             tile(side, keys, values, before, after + t, bounds, offset, count)
             return 0
 
-        lax.fori_loop(begin, tiles if end is None else end, step, 0)
+        if end is None:
+            lax.fori_loop(0, tiles, step, 0)
+        else:
+            for t in range(begin, end):
+                step(t, 0)
         return (
             jnp.where(low == 0, low_before, after + low - 1),
             jnp.where(low == tiles, high_before, after + tiles - 1),
@@ -282,50 +278,102 @@
             share(d, 1 - core).wait_recv()
 
     parts = [arrival[i:i + TILE] for i in range(0, nz, TILE)]
+    ends = {}
+
+    def lists(index):
+        if index == 0:
+            loads[1].wait()
+            own_block.append(layout_ref[2 * z + core])
+        arrange(groups[index])
+
+    def scale_own():
+        loads[0].wait()
+        scaled(plane, q_ref)
+
+    def empty_state():
+        m_s[0] = jnp.full(m_s.shape[1:], EMPTY, jnp.float32)
+        al_s[0] = jnp.zeros(al_s.shape[1:], jnp.float32)
+
+    def relay_on(r):
+        for way in range(2):
+            first(way, r).wait_recv()
+            second(way, r).start()
+
+    def scale_other():
+        for r in range(2):
+            for way in range(2):
+                second(way, r).wait_recv()
+        scaled(1 - plane, qx)
+
+    def upper(index, before, after, chunk):
+        first_part(parts[index], before() if callable(before) else before, after, chunk * per_chunk, per_chunk)
+
+    def picked(index, low_before, high_before, after, t, chunk):
+        low_before = low_before() if callable(low_before) else low_before
+        ends[index] = second_part(
+            index, low_before, high_before, after, chunk * per_chunk, per_chunk, t, t + 1
+        )
+
+    def near_low():
+        return ends[0][0]
+
+    def near_high():
+        return ends[0][1]
+
+    def lower_of(t, chunk):
+        return lambda: picked(1, near_low, 2, 7, t, chunk)
+
+    def near_of(t, chunk):
+        return lambda: picked(0, 0, 1, 3, t, chunk)
+
+    work = {
+        (1, 1): [scale_own],
+        (1, 2): [lambda: lists(0)],
+        (1, 3): [lambda: relay_on(0)],
+        (2, 1): [lambda: lists(1), lambda: lists(2)],
+        (2, 2): [empty_state],
+        (2, 3): [lambda: relay_on(1)],
+        (3, 2): [scale_other],
+        (3, 3): [lambda: shared(1, 2), lambda: upper(0, None, 1, 0)],
+        (4, 1): [lambda: upper(0, None, 1, 1)],
+        (4, 2): [lambda: shared(3), near_of(0, 0)],
+        (4, 3): [near_of(0, 1)],
+        (5, 1): [near_of(1, 0)],
+        (5, 2): [near_of(1, 1)],
+        (5, 3): [near_of(2, 0)],
+        (6, 1): [near_of(2, 1)],
+        (6, 2): [lambda: shared(4), lambda: upper(1, near_high, 2, 0)],
+        (6, 3): [lambda: upper(1, near_high, 2, 1)],
+        (7, 1): [lambda: shared(5), lower_of(0, 0)],
+        (7, 2): [lower_of(0, 1)],
+        (7, 3): [
+            lower_of(1, 0), lower_of(1, 1), lambda: shared(6),
+            lambda: upper(2, lambda: ends[1][1], 6, 0), lambda: upper(2, lambda: ends[1][1], 6, 1),
+        ],
+    }
+
     for d in range(1, last + 1):
         for b in range(2):
-            if d < last - 1:
-                for g in range(2):
+            for g in range(2):
+                if d < last:
                     ring(d, b, g).wait_recv()
-                    ring(d + 1, b, g).start()
-            elif d == last - 1:
-                for g in range(2):
-                    ring(d, b, g).wait_recv()
-
-                @pl.when(core == b)
-                def _():
-                    for g in range(2):
-                        ring(last, b, g).start()
-            else:
-
-                @pl.when(core == b)
-                def _():
-                    for g in range(2):
+                    if d + 1 < last:
+                        ring(d + 1, b, g).start()
+                    else:
+
+                        @pl.when(core == b)
+                        def _():
+                            ring(last, b, g).start()
+                else:
+
+                    @pl.when(core == b)
+                    def _():
                         ring(last, b, g).wait_recv()
-        share(d, core).start()
-        if d <= 2:
-            for way in range(2):
-                first(way, d - 1).wait_recv()
-                second(way, d - 1).start()
-        if d == 3:
-            for r in range(2):
-                for way in range(2):
-                    second(way, r).wait_recv()
-            scaled(1 - plane, qx)
-            shared(1, 2)
-            first_part(parts[0], None, 1, 0, group)
-        if d == 4:
-            shared(3)
-            second_part(0, 0, 1, 3, 0, group, 0, 2)
-        if d == 5:
-            low_at, high_at = second_part(0, 0, 1, 3, 0, group, 2, 3)
-        if d == 6:
-            shared(4)
-            first_part(parts[1], high_at, 2, 0, group)
-        if d == 7:
-            shared(5, 6)
-            first_part(parts[2], 2, 6, 0, group)
-            low_at, high_at = second_part(1, low_at, 6, 7, 0, group)
+                if (b, g) == (1, 1):
+                    share(d, core).start()
+                for task in work.get((d, 2 * b + g), ()):
+                    task()
+    low_at, high_at = ends[1][0], 6
     shared(last - 1, last)
 
     lane = lax.broadcasted_iota(jnp.int32, (tok, HEAD_SIZE), 1)

time: 61.1 us -> 62.1 us (1.016)
  Pallas kernels: 59.3 us -> 60.3 us
    pallas_call x1, Pallas kernels: 59.3 us -> 60.3 us  [per_device(): pl.pallas_call(lambda *refs: kernel(nz, heads, arrival, groups, *refs), o...]
where the time goes in v4:
time: 62.1 us; the launch traced here: 62 us
  Pallas kernels  60.3 us (97%)
  local copies, waits for them, and re-layouts  1.67 us (3%)
    pallas_call x1, Pallas kernels, per_device(): pl.pallas_call(lambda *refs: kernel(nz, heads, arrival, groups, *refs), o...  60.3 us
    unnamed x1, local copies, waits for them, and re-layouts  1.67 us

profile of v4, /device:TPU:1, one launch (start us, length us, event | category | flops | bytes accessed | tf_op | source)
XLA Modules:
  0.0 62.0 jit_solution(900494362958339132)
XLA Ops:
  0.0 60.3 %shard_map.46 = bf16[16,8192]{1,0:T(8,128)(2,1)} custom-call(s32[64]{0:T(128)} %refs_0_.1, bf16[128,1024]{1,0:T(8,128)(2,1)} %refs_1_.1, bf16[128,128]{1,0:T(8,128)(2,1)} %refs_2_.1, bf16[128,128]{1,0:T(8,128)(2,1)} %refs_3_.1), custom_call_target="tpu_custom_call" | custom-call | flops 2281701376 | bytes 524288 | tf_op jit(solution)/shard_map/pallas_call | solution.py:489
  60.3 1.7 %copy.6 = bf16[16,8192]{1,0:T(8,128)(2,1)} copy(bf16[16,8192]{1,0:T(8,128)(2,1)} %shard_map.46) | data formatting | bytes 524288

commit v5 on v4

--- a/solution.py
+++ b/solution.py
@@ -86,7 +86,7 @@
 
     def granule(d, b, g):
         buffer, n = spot(d, core)
-        return buffer.at[n, sides[b], g]
+        return buffer.at[n, sides[b], g if b == 0 else (core + g) % 2]
 
     def own(g):
         return pltpu.make_async_copy((k_ref, v_ref)[g], granule(0, 0, g), local.at[g])
@@ -123,13 +123,14 @@
     def home(g):
         return send((k_ref, v_ref)[g], granule(0, 0, g), cross_send.at[0, g], cross_recv.at[0, g], sibling)
 
-    def abroad(cc, g):
-        return send(
-            (k_ref, v_ref)[g], granule(0, 0, g), cross_send.at[cc, g], cross_recv.at[1, g], opposite[cc]
-        )
-
-    def from_abroad(g):
-        return send((k_ref, v_ref)[g], granule(0, 1, g), cross_send.at[1, g], cross_recv.at[1, g], opposite[0])
+    def abroad(g):
+        return send((k_ref, v_ref)[g], kv_0.at[0, plane, g], cross_send.at[0, g], cross_recv.at[1, 0], opposite[g])
+
+    def pass_on():
+        return send(granule(0, 1, 0), granule(0, 1, 0), cross_send.at[1, 0], cross_recv.at[1, 1], sibling)
+
+    def passed():
+        return send(granule(0, 1, 1), granule(0, 1, 1), cross_send.at[1, 0], cross_recv.at[1, 1], sibling)
 
     half, strip = width // 2, tok // 2
 
@@ -144,8 +145,7 @@
     @pl.when(core != plane)
     def _():
         for g in range(2):
-            for cc in range(2):
-                abroad(cc, g).start()
+            abroad(g).start()
 
     @pl.when(core == plane)
     def _():
@@ -163,12 +163,14 @@
             own(g).wait()
 
         ring(1, 0, g).start()
+    send(k_ref, granule(0, 1, 0), cross_send.at[0, 0], cross_recv.at[1, 0], opposite[0]).wait_recv()
+    ring(1, 1, 0).start()
+    pass_on().start()
     for r in range(2):
         for way in range(2):
             first(way, r).start()
-    for g in range(2):
-        from_abroad(g).wait_recv()
-        ring(1, 1, g).start()
+    passed().wait_recv()
+    ring(1, 1, 1).start()
 
     own_block, low_tiles, starts, tile_counts = [], [], [], []
 
@@ -263,11 +265,7 @@
             tile(side, keys, values, before, after + t, bounds, offset, count)
             return 0
 
-        if end is None:
-            lax.fori_loop(0, tiles, step, 0)
-        else:
-            for t in range(begin, end):
-                step(t, 0)
+        lax.fori_loop(begin, tiles if end is None else end, step, 0)
         return (
             jnp.where(low == 0, low_before, after + low - 1),
             jnp.where(low == tiles, high_before, after + tiles - 1),
@@ -305,51 +303,20 @@
                 second(way, r).wait_recv()
         scaled(1 - plane, qx)
 
-    def upper(index, before, after, chunk):
-        first_part(parts[index], before() if callable(before) else before, after, chunk * per_chunk, per_chunk)
-
-    def picked(index, low_before, high_before, after, t, chunk):
-        low_before = low_before() if callable(low_before) else low_before
-        ends[index] = second_part(
-            index, low_before, high_before, after, chunk * per_chunk, per_chunk, t, t + 1
-        )
-
-    def near_low():
-        return ends[0][0]
-
-    def near_high():
-        return ends[0][1]
-
-    def lower_of(t, chunk):
-        return lambda: picked(1, near_low, 2, 7, t, chunk)
-
-    def near_of(t, chunk):
-        return lambda: picked(0, 0, 1, 3, t, chunk)
+    def near(begin, end):
+        ends[0] = second_part(0, 0, 1, 3, 0, group, begin, end)
+
+    def middle():
+        ends[1] = second_part(1, ends[0][0], 2, 7, 0, group)
 
     work = {
-        (1, 1): [scale_own],
-        (1, 2): [lambda: lists(0)],
-        (1, 3): [lambda: relay_on(0)],
-        (2, 1): [lambda: lists(1), lambda: lists(2)],
-        (2, 2): [empty_state],
-        (2, 3): [lambda: relay_on(1)],
-        (3, 2): [scale_other],
-        (3, 3): [lambda: shared(1, 2), lambda: upper(0, None, 1, 0)],
-        (4, 1): [lambda: upper(0, None, 1, 1)],
-        (4, 2): [lambda: shared(3), near_of(0, 0)],
-        (4, 3): [near_of(0, 1)],
-        (5, 1): [near_of(1, 0)],
-        (5, 2): [near_of(1, 1)],
-        (5, 3): [near_of(2, 0)],
-        (6, 1): [near_of(2, 1)],
-        (6, 2): [lambda: shared(4), lambda: upper(1, near_high, 2, 0)],
-        (6, 3): [lambda: upper(1, near_high, 2, 1)],
-        (7, 1): [lambda: shared(5), lower_of(0, 0)],
-        (7, 2): [lower_of(0, 1)],
-        (7, 3): [
-            lower_of(1, 0), lower_of(1, 1), lambda: shared(6),
-            lambda: upper(2, lambda: ends[1][1], 6, 0), lambda: upper(2, lambda: ends[1][1], 6, 1),
-        ],
+        1: [scale_own, lambda: lists(0)],
+        2: [lambda: relay_on(0), lambda: lists(1), lambda: lists(2), empty_state],
+        3: [lambda: relay_on(1)],
+        4: [scale_other, lambda: shared(1, 2), lambda: first_part(parts[0], None, 1, 0, group)],
+        5: [lambda: shared(3), lambda: near(0, 2)],
+        6: [lambda: near(2, 3), lambda: shared(4), lambda: first_part(parts[1], ends[0][1], 2, 0, group)],
+        7: [lambda: shared(5), middle, lambda: shared(6), lambda: first_part(parts[2], ends[1][1], 6, 0, group)],
     }
 
     for d in range(1, last + 1):
@@ -371,8 +338,8 @@
                         ring(last, b, g).wait_recv()
                 if (b, g) == (1, 1):
                     share(d, core).start()
-                for task in work.get((d, 2 * b + g), ()):
-                    task()
+        for task in work.get(d, ()):
+            task()
     low_at, high_at = ends[1][0], 6
     shared(last - 1, last)
 
@@ -406,7 +373,11 @@
                 )
                 level = jnp.where(some, m + jnp.log2(safe), EMPTY)
                 lse[side] = jnp.where(lax.rem(lane, group) == offset + n, level, lse[side])
-        spread(out_send.at[chunk], out_recv.at[chunk], chunk)
+
+        @pl.when(chunk < CHUNKS - 1)
+        def _():
+            spread(out_send.at[chunk], out_recv.at[chunk], chunk)
+
         return 0
 
     lax.fori_loop(0, CHUNKS, chunk_step, 0)
@@ -419,6 +390,7 @@
         packed = jnp.where(lane < group, high, jnp.where(lane < 2 * group, rest, low)).astype(jnp.bfloat16)
         stat_send[side * heads:(side + 1) * heads] = packed.reshape(heads, piece, HEAD_SIZE)
     spread(stat_send, stat_recv, CHUNKS)
+    spread(out_send.at[CHUNKS - 1], out_recv.at[CHUNKS - 1], CHUNKS - 1)
 
     for d in range(1, last + 1):
         share(d, core).wait_send()
@@ -426,8 +398,7 @@
 
         @pl.when(core != plane)
         def _():
-            for cc in range(2):
-                abroad(cc, g).wait_send()
+            abroad(g).wait_send()
 
         @pl.when(core == plane)
         def _():
@@ -440,15 +411,14 @@
             @pl.when(core == b)
             def _():
                 ring(last, b, g).wait_send()
+    pass_on().wait_send()
     for r in range(2):
         for way in range(2):
             first(way, r).wait_send()
             second(way, r).wait_send()
 
     pltpu.make_async_copy(stat_send, stat_recv, o_recv.at[CHUNKS]).wait()
-    for chunk in range(CHUNKS):
-        pltpu.make_async_copy(out_send.at[chunk], out_recv.at[chunk], o_recv.at[chunk]).wait()
-
+    portions = []
     for source in range(heads):
         levels = []
         for side in range(2):
@@ -456,15 +426,18 @@
             levels.append(
                 packed + pltpu.roll(packed, HEAD_SIZE - group, 1) + pltpu.roll(packed, HEAD_SIZE - 2 * group, 1)
             )
-        share_0 = 1.0 / (1.0 + jnp.exp2(levels[1] - levels[0]))
-        for head in range(group):
-            chunk, n = head // per_chunk, head % per_chunk
-            columns = slice(n * HEAD_SIZE, (n + 1) * HEAD_SIZE)
-            part_0 = out_recv[chunk, source, :, columns].astype(jnp.float32)
-            part_1 = out_recv[chunk, heads + source, :, columns].astype(jnp.float32)
-            portion = jnp.broadcast_to(share_0[:, head:head + 1], (piece, HEAD_SIZE))
-            start = (source * group + head) * HEAD_SIZE
-            out_ref[:, start:start + HEAD_SIZE] = (part_1 + portion * (part_0 - part_1)).astype(jnp.bfloat16)
+        portions.append(1.0 / (1.0 + jnp.exp2(levels[1] - levels[0])))
+    for chunk in range(CHUNKS):
+        pltpu.make_async_copy(out_send.at[chunk], out_recv.at[chunk], o_recv.at[chunk]).wait()
+        for source in range(heads):
+            for n in range(per_chunk):
+                head = chunk * per_chunk + n
+                columns = slice(n * HEAD_SIZE, (n + 1) * HEAD_SIZE)
+                part_0 = out_recv[chunk, source, :, columns].astype(jnp.float32)
+                part_1 = out_recv[chunk, heads + source, :, columns].astype(jnp.float32)
+                portion = jnp.broadcast_to(portions[source][:, head:head + 1], (piece, HEAD_SIZE))
+                start = (source * group + head) * HEAD_SIZE
+                out_ref[:, start:start + HEAD_SIZE] = (part_1 + portion * (part_0 - part_1)).astype(jnp.bfloat16)
 
     others = pl.ds(0, 2 * heads - 1)
     pltpu.make_async_copy(stat_send.at[others], stat_recv.at[others], o_send.at[CHUNKS]).wait()
@@ -484,12 +457,12 @@
         entries = sum(tiles_for(slots) for slots in groups) * TILE
         states = 1 + nz // TILE + entries // TILE
         bf16, f32, dma = jnp.bfloat16, jnp.float32, pltpu.SemaphoreType.DMA
-        anywhere = pl.BlockSpec(memory_space=pl.ANY)
+        hbm = pl.BlockSpec(memory_space=pltpu.HBM)
 
         return pl.pallas_call(
             lambda *refs: kernel(nz, heads, arrival, groups, *refs),
             out_shape=jax.ShapeDtypeStruct((piece, heads * width), bf16),
-            in_specs=[anywhere] * 4,
+            in_specs=[hbm] * 4,
             out_specs=pl.BlockSpec(memory_space=pltpu.VMEM),
             scratch_shapes=[pltpu.VMEM((len(slots), 2, 2, tok, HEAD_SIZE), bf16) for slots in groups]
             + [
@@ -513,14 +486,14 @@
                 dma((CHUNKS + 1,)), dma((CHUNKS + 1,)), dma((4,)),
             ],
             compiler_params=pltpu.CompilerParams(
-                collective_id=0, has_side_effects=True, vmem_limit_bytes=60 * 1024 * 1024
+                collective_id=0, has_side_effects=True, vmem_limit_bytes=44 * 1024 * 1024
             ),
             cost_estimate=pl.CostEstimate(
                 flops=4 * 2 * (nz + 1) * tok * group * tok * HEAD_SIZE,
                 bytes_accessed=4 * tok * width,
                 transcendentals=2 * (nz + 1) * tok * group * tok,
             ),
-        )(layout, queries, keys, values)
+        )(*(pltpu.with_memory_space_constraint(a, pltpu.HBM) for a in (layout, queries, keys, values)))
 
     return jax.shard_map(
         per_device,

time: 62.1 us -> 59.1 us (0.952)
  Pallas kernels: 60.3 us -> 58.3 us
  local copies, waits for them, and re-layouts: 1.67 us -> 0.71 us
    pallas_call x1, Pallas kernels: 60.3 us -> 58.3 us  [per_device(): pl.pallas_call(lambda *refs: kernel(nz, heads, arrival, groups, *refs), o...]
    unnamed x1, local copies, waits for them, and re-layouts: 1.67 us -> 0.71 us
where the time goes in v5:
time: 59.1 us; the launch traced here: 59 us
  Pallas kernels  58.3 us (99%)
  local copies, waits for them, and re-layouts  0.71 us (1%)
    pallas_call x1, Pallas kernels, per_device(): pl.pallas_call(lambda *refs: kernel(nz, heads, arrival, groups, *refs), o...  58.3 us

profile of v5, /device:TPU:1, one launch (start us, length us, event | category | flops | bytes accessed | tf_op | source)
XLA Modules:
  0.0 59.0 jit_solution(7375579014348452200)
XLA Ops:
  0.0 58.3 %shard_map.46 = bf16[16,8192]{1,0:T(8,128)(2,1)S(1)} custom-call(s32[64]{0:T(128)} %refs_0_.1, bf16[128,1024]{1,0:T(8,128)(2,1)} %refs_1_.1, bf16[128,128]{1,0:T(8,128)(2,1)} %refs_2_.1, bf16[128,128]{1,0:T(8,128)(2,1)} %refs_3_.1), custom_call_target="tpu_custom_call" | custom-call | flops 2281701376 | bytes 524288 | tf_op jit(solution)/shard_map/pallas_call | solution.py:462
  58.3 0.7 %copy.6 = bf16[16,8192]{1,0:T(8,128)(2,1)} copy(bf16[16,8192]{1,0:T(8,128)(2,1)S(1)} %shard_map.46) | data formatting | bytes 524288

commit v6 on v5

--- a/solution.py
+++ b/solution.py
@@ -33,18 +33,16 @@
 
 def kernel(
     nz, heads, arrival, groups, layout_hbm, q_hbm, k_ref, v_ref, out_ref,
-    kv_0, kv_1, kv_2, q_ref, qx, relay, qs, m_s, al_s, out_send, out_recv, stat_send, stat_recv, lse,
+    kv_0, kv_1, kv_2, q_ref, qx, qs, m_s, al_s, out_send, out_recv, stat_send, stat_recv, lse,
     layout_ref, pick, limit, place,
     ring_send, ring_recv, share_send, share_recv, cross_send, cross_recv,
-    first_send, first_recv, second_send, second_recv, o_send, o_recv, local,
+    first_send, first_recv, o_send, o_recv, local,
 ):
     tok, width = q_ref.shape
     group = width // HEAD_SIZE
     per_chunk = group // CHUNKS
     piece = tok // heads
     plane, z, core, h = places(nz, heads)
-    nx = heads // 2
-    y_lo, x = h // nx, h % nx
     last = nz // 2
 
     def at(p, zz, cc):
@@ -54,11 +52,11 @@
     onward, backward = (at(plane, (z + step_to) % nz, core), h), (at(plane, (z + nz - step_to) % nz, core), h)
     sibling = (at(plane, z, 1 - core), h)
     opposite = [(at(1 - plane, z, cc), h) for cc in range(2)]
-    above = (at((plane + y_lo) % 2, z, core), (1 - y_lo) * nx + x)
-    below = (at((plane + 1 - y_lo) % 2, z, core), (1 - y_lo) * nx + x)
+    partner = (at(1 - plane, z, core), h)
 
     def outward(e):
-        return (plane + e // heads) % 2, (h + e % heads) % heads
+        y, half, x = (h // 4 + e // 4) % 2, (h // 2 + e // 2) % 2, (h + e) % 2
+        return (plane + e // 8) % 2, y * 4 + half * 2 + x
 
     def device(e):
         p, j = outward(e)
@@ -132,15 +130,8 @@
     def passed():
         return send(granule(0, 1, 1), granule(0, 1, 1), cross_send.at[1, 0], cross_recv.at[1, 1], sibling)
 
-    half, strip = width // 2, tok // 2
-
-    def first(way, r):
-        src = q_hbm.at[pl.ds(r * strip, strip), pl.ds(way * half, half)]
-        return send(src, relay.at[way, r], first_send.at[way, r], first_recv.at[way, r], (above, below)[way])
-
-    def second(way, r):
-        dst = qx.at[pl.ds(r * strip, strip), pl.ds(way * half, half)]
-        return send(relay.at[way, r], dst, second_send.at[way, r], second_recv.at[way, r], (above, below)[way])
+    def hand_over():
+        return send(q_hbm, qx, first_send.at[0], first_recv.at[0], partner)
 
     @pl.when(core != plane)
     def _():
@@ -166,9 +157,7 @@
     send(k_ref, granule(0, 1, 0), cross_send.at[0, 0], cross_recv.at[1, 0], opposite[0]).wait_recv()
     ring(1, 1, 0).start()
     pass_on().start()
-    for r in range(2):
-        for way in range(2):
-            first(way, r).start()
+    hand_over().start()
     passed().wait_recv()
     ring(1, 1, 1).start()
 
@@ -292,15 +281,8 @@
         m_s[0] = jnp.full(m_s.shape[1:], EMPTY, jnp.float32)
         al_s[0] = jnp.zeros(al_s.shape[1:], jnp.float32)
 
-    def relay_on(r):
-        for way in range(2):
-            first(way, r).wait_recv()
-            second(way, r).start()
-
     def scale_other():
-        for r in range(2):
-            for way in range(2):
-                second(way, r).wait_recv()
+        hand_over().wait_recv()
         scaled(1 - plane, qx)
 
     def near(begin, end):
@@ -311,8 +293,8 @@
 
     work = {
         1: [scale_own, lambda: lists(0)],
-        2: [lambda: relay_on(0), lambda: lists(1), lambda: lists(2), empty_state],
-        3: [lambda: relay_on(1)],
+        2: [lambda: lists(1), lambda: lists(2)],
+        3: [empty_state],
         4: [scale_other, lambda: shared(1, 2), lambda: first_part(parts[0], None, 1, 0, group)],
         5: [lambda: shared(3), lambda: near(0, 2)],
         6: [lambda: near(2, 3), lambda: shared(4), lambda: first_part(parts[1], ends[0][1], 2, 0, group)],
@@ -345,7 +327,7 @@
 
     lane = lax.broadcasted_iota(jnp.int32, (tok, HEAD_SIZE), 1)
     mine = plane * heads + h
-    far_first = sorted(range(1, 2 * heads), key=lambda e: (e % heads) not in (0, 2, 6))
+    far_first = sorted(range(1, 2 * heads), key=lambda e: -(e // 8 + e // 2 % 2))
 
     def spread(buffer, landing, index):
         for e in far_first:
@@ -412,10 +394,7 @@
             def _():
                 ring(last, b, g).wait_send()
     pass_on().wait_send()
-    for r in range(2):
-        for way in range(2):
-            first(way, r).wait_send()
-            second(way, r).wait_send()
+    hand_over().wait_send()
 
     pltpu.make_async_copy(stat_send, stat_recv, o_recv.at[CHUNKS]).wait()
     portions = []
@@ -468,7 +447,6 @@
             + [
                 pltpu.VMEM((tok, width), bf16),
                 pltpu.VMEM((tok, width), bf16),
-                pltpu.VMEM((2, 2, tok // 2, width // 2), bf16),
                 pltpu.VMEM((2, group, tok, HEAD_SIZE), bf16),
                 pltpu.VMEM((states, group, tok, HEAD_SIZE), f32),
                 pltpu.VMEM((states, group, tok, 2 * HEAD_SIZE), f32),
@@ -482,7 +460,7 @@
                 pltpu.SMEM((entries,), jnp.int32),
                 pltpu.SMEM((3, 2 * TILE), jnp.int32),
                 dma((nz // 2, 2, 2)), dma((nz // 2, 2, 2)), dma((nz // 2,)), dma((nz // 2,)), dma((2, 2)), dma((2, 2)),
-                dma((2, 2)), dma((2, 2)), dma((2, 2)), dma((2, 2)),
+                dma((1,)), dma((1,)),
                 dma((CHUNKS + 1,)), dma((CHUNKS + 1,)), dma((4,)),
             ],
             compiler_params=pltpu.CompilerParams(

time: 59.1 us -> 58.4 us (0.988)
  Pallas kernels: 58.3 us -> 57.6 us
    pallas_call x1, Pallas kernels: 58.3 us -> 57.6 us  [per_device(): pl.pallas_call(lambda *refs: kernel(nz, heads, arrival, groups, *refs), o...]
where the time goes in v6:
time: 58.4 us; the launch traced here: 58.3 us
  Pallas kernels  57.6 us (99%)
  local copies, waits for them, and re-layouts  0.71 us (1%)
    pallas_call x1, Pallas kernels, per_device(): pl.pallas_call(lambda *refs: kernel(nz, heads, arrival, groups, *refs), o...  57.6 us

profile of v6, /device:TPU:1, one launch (start us, length us, event | category | flops | bytes accessed | tf_op | source)
XLA Modules:
  0.0 58.3 jit_solution(18244220703676564038)
XLA Ops:
  0.0 57.6 %shard_map.46 = bf16[16,8192]{1,0:T(8,128)(2,1)S(1)} custom-call(s32[64]{0:T(128)} %refs_0_.1, bf16[128,1024]{1,0:T(8,128)(2,1)} %refs_1_.1, bf16[128,128]{1,0:T(8,128)(2,1)} %refs_2_.1, bf16[128,128]{1,0:T(8,128)(2,1)} %refs_3_.1), custom_call_target="tpu_custom_call" | custom-call | flops 2281701376 | bytes 524288 | tf_op jit(solution)/shard_map/pallas_call | solution.py:441
  57.6 0.7 %copy.6 = bf16[16,8192]{1,0:T(8,128)(2,1)} copy(bf16[16,8192]{1,0:T(8,128)(2,1)S(1)} %shard_map.46) | data formatting | bytes 524288

commit v7 on v6

--- a/solution.py
+++ b/solution.py
@@ -12,7 +12,7 @@
 MESH = pl.DeviceIdType.MESH
 EMPTY = -1e30
 SCALE = math.log2(math.e) / math.sqrt(HEAD_SIZE)
-CHUNKS = 2
+CHUNKS = 4
 TILE = 4
 
 

time: 58.4 us -> 58.6 us (level)
  no operation moved by 1% of the time
where the time goes in v7:
time: 58.6 us; the launch traced here: 58.5 us
  Pallas kernels  57.7 us (98%)
  local copies, waits for them, and re-layouts  0.71 us (1%)
    pallas_call x1, Pallas kernels, per_device(): pl.pallas_call(lambda *refs: kernel(nz, heads, arrival, groups, *refs), o...  57.7 us

profile of v7, /device:TPU:1, one launch (start us, length us, event | category | flops | bytes accessed | tf_op | source)
XLA Modules:
  0.0 58.5 jit_solution(5882986425437121652)
XLA Ops:
  0.0 57.7 %shard_map.46 = bf16[16,8192]{1,0:T(8,128)(2,1)S(1)} custom-call(s32[64]{0:T(128)} %refs_0_.1, bf16[128,1024]{1,0:T(8,128)(2,1)} %refs_1_.1, bf16[128,128]{1,0:T(8,128)(2,1)} %refs_2_.1, bf16[128,128]{1,0:T(8,128)(2,1)} %refs_3_.1), custom_call_target="tpu_custom_call" | custom-call | flops 2281701376 | bytes 524288 | tf_op jit(solution)/shard_map/pallas_call | solution.py:441
  57.8 0.7 %copy.6 = bf16[16,8192]{1,0:T(8,128)(2,1)} copy(bf16[16,8192]{1,0:T(8,128)(2,1)S(1)} %shard_map.46) | data formatting | bytes 524288

commit v8 on v7

--- a/solution.py
+++ b/solution.py
@@ -154,10 +154,10 @@
             own(g).wait()
 
         ring(1, 0, g).start()
+    hand_over().start()
     send(k_ref, granule(0, 1, 0), cross_send.at[0, 0], cross_recv.at[1, 0], opposite[0]).wait_recv()
     ring(1, 1, 0).start()
     pass_on().start()
-    hand_over().start()
     passed().wait_recv()
     ring(1, 1, 1).start()
 
@@ -293,12 +293,12 @@
 
     work = {
         1: [scale_own, lambda: lists(0)],
-        2: [lambda: lists(1), lambda: lists(2)],
-        3: [empty_state],
-        4: [scale_other, lambda: shared(1, 2), lambda: first_part(parts[0], None, 1, 0, group)],
-        5: [lambda: shared(3), lambda: near(0, 2)],
-        6: [lambda: near(2, 3), lambda: shared(4), lambda: first_part(parts[1], ends[0][1], 2, 0, group)],
-        7: [lambda: shared(5), middle, lambda: shared(6), lambda: first_part(parts[2], ends[1][1], 6, 0, group)],
+        2: [lambda: lists(1), lambda: lists(2), empty_state],
+        3: [scale_other, lambda: shared(1, 2), lambda: first_part(parts[0], None, 1, 0, group)],
+        4: [lambda: shared(3), lambda: near(0, 2)],
+        5: [lambda: near(2, 3), lambda: shared(4), lambda: first_part(parts[1], ends[0][1], 2, 0, group)],
+        6: [lambda: shared(5), middle],
+        7: [lambda: shared(6), lambda: first_part(parts[2], ends[1][1], 6, 0, group)],
     }
 
     for d in range(1, last + 1):

time: 58.6 us -> 58.7 us (level)
  no operation moved by 1% of the time
where the time goes in v8:
time: 58.7 us; the launch traced here: 58.6 us
  Pallas kernels  57.9 us (99%)
  local copies, waits for them, and re-layouts  0.71 us (1%)
    pallas_call x1, Pallas kernels, per_device(): pl.pallas_call(lambda *refs: kernel(nz, heads, arrival, groups, *refs), o...  57.9 us

profile of v8, /device:TPU:1, one launch (start us, length us, event | category | flops | bytes accessed | tf_op | source)
XLA Modules:
  0.0 58.6 jit_solution(12984758048719526399)
XLA Ops:
  0.0 57.9 %shard_map.46 = bf16[16,8192]{1,0:T(8,128)(2,1)S(1)} custom-call(s32[64]{0:T(128)} %refs_0_.1, bf16[128,1024]{1,0:T(8,128)(2,1)} %refs_1_.1, bf16[128,128]{1,0:T(8,128)(2,1)} %refs_2_.1, bf16[128,128]{1,0:T(8,128)(2,1)} %refs_3_.1), custom_call_target="tpu_custom_call" | custom-call | flops 2281701376 | bytes 524288 | tf_op jit(solution)/shard_map/pallas_call | solution.py:441
  57.9 0.7 %copy.6 = bf16[16,8192]{1,0:T(8,128)(2,1)} copy(bf16[16,8192]{1,0:T(8,128)(2,1)S(1)} %shard_map.46) | data formatting | bytes 524288
